TPU v7x, 512 devices: a whole 4x8x8 slice. The times are simulated.
512 devices in a mesh: district: 16 (over y, core), tile: 32 (over z, x).
Axes of the slice: x: 4, y: 8, z: 8, core: 2. Of those that a mesh axis runs over, the one named last changes fastest.
Arguments:
- features: bfloat16 [2048, 96, 128], P(('district', 'tile')), may hold values from -6 to 6
- pre_act: bfloat16 [2048, 96, 128], P(('district', 'tile')), may hold values from -6 to 6
- out_grad: bfloat16 [2048, 96, 128], P(('district', 'tile')), may hold values from -6 to 6
- weight_one: bfloat16 [27, 96, 96], replicated, may hold values from -0.15625 to 0.15625
- weight_two: bfloat16 [27, 96, 96], replicated, may hold values from -0.15625 to 0.15625
- block_count: int32 [512], P(('district', 'tile')), may hold values from 1 to 4, as said below
- pair_in: int32 [512, 64], P(('district', 'tile')), may hold values from 0 to 11, as said below
- pair_off: int32 [512, 64], P(('district', 'tile')), may hold values from 0 to 26
- row_map: int32 [512, 64, 128], P(('district', 'tile')), may hold values from 0 to 159
- send_lo: int32 [512, 4], P(('district', 'tile')), may hold values from 0 to 3, as said below
- send_hi: int32 [512, 4], P(('district', 'tile')), may hold values from 0 to 3, as said below
Outputs:
- feature_grad: bfloat16 [2048, 96, 128], P(('district', 'tile'))
- grad_one: float32 [27, 96, 96], replicated
- grad_two: float32 [27, 96, 96], replicated
Inputs may be any that keep to these rules, and one draw needn't show every extreme that they name: `block_count`: at most 4, reached by some tile in every draw; at least 1. `pair_in`: an index of the tile's extended list: below its block_count (own blocks), or 4 to 11. `row_map`: values of 128 or more mean no input voxel. `send_lo`: active blocks of the sending tile, below its block_count; repeats possible. `send_hi`: active blocks of the sending tile, below its block_count; repeats possible.
All inputs are finite; a program needn't handle non-finite values.
Results may differ from a plain program's by a relative error of at most 0.0049.
Values may be sent and summed in bfloat16 or wider, within the bound.
A program may use at most 64 MiB of HBM per device.

v0:
```python
import math

import jax
import jax.numpy as jnp
from jax import lax
from jax.sharding import PartitionSpec as P

K = 27
PB = 16


def passed_along(block, axis, distance):
    devices = range(lax.axis_size(axis))
    route = [(i - distance, i) for i in devices if i - distance in devices]
    return lax.ppermute(block, axis, route)


def extend(stacked, send_lo, send_hi):
    lower_part = stacked[send_lo]
    upper_part = stacked[send_hi]
    from_lower = passed_along(upper_part, "tile", 1)
    from_upper = passed_along(lower_part, "tile", -1)
    return jnp.concatenate([stacked, from_lower, from_upper], axis=0)


def give_back(dext, blocks, send_lo, send_hi):
    width = send_lo.shape[0]
    local = dext[:blocks]
    low = dext[blocks : blocks + width]
    high = dext[blocks + width :]
    for_lo = passed_along(high, "tile", 1)
    for_hi = passed_along(low, "tile", -1)
    return local.at[send_lo].add(for_lo).at[send_hi].add(for_hi)


def layer_back(ext, output_gradient, kernel_weight, count, pair_in, pair_off, row_map):
    ext_blocks, chans, rows = ext.shape
    blocks = output_gradient.shape[0]
    group = PB * math.gcd(blocks, 4)
    out_per = group // PB
    trash = ext_blocks * rows
    flat_in = jnp.concatenate(
        [jnp.transpose(ext, (1, 0, 2)).reshape(chans, trash), jnp.zeros((chans, rows), ext.dtype)],
        axis=1,
    )
    table = kernel_weight.reshape(K, chans * chans)
    offsets = jnp.arange(K, dtype=jnp.int32)

    def step(index, carry):
        dflat, dweight = carry
        start = index * group
        pidx = start + jnp.arange(group, dtype=jnp.int32)
        live = pidx // PB < count
        valid = (row_map < rows) & live[:, None]
        flat_idx = jnp.where(valid, pair_in[:, None] * rows + row_map, trash)
        gathered_input_rows = flat_in[:, flat_idx].reshape(chans, out_per, PB, rows)
        dweight_pairs = jnp.einsum(
            "cosr,odr->oscd",
            gathered_input_rows,
            output_gradient,
            preferred_element_type=jnp.float32,
        )
        dweight_pairs = dweight_pairs.reshape(group, chans * chans)
        onehot = pair_off[:, None] == offsets[None, :]
        summed = jnp.sum(jnp.where(onehot[:, :, None], dweight_pairs[:, None, :], 0.0), axis=0)
        dweight = dweight + summed.reshape(K, chans, chans)
        wpairs = jnp.dot(onehot.astype(jnp.bfloat16), table, preferred_element_type=jnp.float32)
        wpairs = wpairs.astype(jnp.bfloat16).reshape(out_per, PB, chans, chans)
        gathered_grad_rows = jnp.einsum(
            "oscd,odr->cosr", wpairs, output_gradient, preferred_element_type=jnp.float32
        )
        dflat = dflat.at[:, flat_idx.reshape(-1)].add(
            gathered_grad_rows.reshape(chans, group * rows)
        )
        return (dflat, dweight)

    turns = (count * PB + group - 1) // group
    init = (
        jnp.zeros((chans, trash + rows), jnp.float32),
        jnp.zeros((K, chans, chans), jnp.float32),
    )
    dflat, dweight = lax.fori_loop(0, turns, step, init)
    dext = jnp.transpose(dflat[:, :trash].reshape(chans, ext_blocks, rows), (1, 0, 2))
    return (dext, dweight)


def body(
    features,
    pre_act,
    out_grad,
    weight_one,
    weight_two,
    block_count,
    pair_in,
    pair_off,
    row_map,
    send_lo,
    send_hi,
):
    blocks = features.shape[0]
    count = block_count[0]
    pin = pair_in[0]
    pair_offset_table = pair_off[0]
    rmap = row_map[0]
    lows = send_lo[0]
    highs = send_hi[0]
    hidden = jnp.maximum(pre_act, jnp.zeros_like(pre_act))
    stacked = jnp.stack([features, hidden], axis=1)
    extended = extend(stacked, lows, highs)
    ext_x = extended[:, 0]
    ext_h = extended[:, 1]
    dext_h, grad_two = layer_back(ext_h, out_grad, weight_two, count, pin, pair_offset_table, rmap)
    hidden_grad = give_back(dext_h, blocks, lows, highs)
    act_grad = jnp.where(pre_act > 0, hidden_grad, 0.0).astype(jnp.bfloat16)
    dext_x, grad_one = layer_back(ext_x, act_grad, weight_one, count, pin, pair_offset_table, rmap)
    feature_grad = give_back(dext_x, blocks, lows, highs).astype(jnp.bfloat16)
    grad_one, grad_two = lax.psum((grad_one, grad_two), ("district", "tile"))
    return (feature_grad, grad_one, grad_two)


def solution(mesh):
    placed = (
        P(("district", "tile"), None, None),
        P(("district", "tile"), None, None),
        P(("district", "tile"), None, None),
        P(),
        P(),
        P(("district", "tile")),
        P(("district", "tile"), None),
        P(("district", "tile"), None),
        P(("district", "tile"), None, None),
        P(("district", "tile"), None),
        P(("district", "tile"), None),
    )
    return jax.shard_map(
        body,
        mesh=mesh,
        in_specs=placed,
        out_specs=(P(("district", "tile"), None, None), P(), P()),
        check_vma=False,
    )
```

profile of v0, /device:TPU:1, one launch (start us, length us, event | category | flops | bytes accessed | tf_op | source)
XLA Modules:
  0.0 610.8 jit_solution(5856157847733811603)
XLA Ops:
  7.2 0.9 maximum_bitcast_fusion
  8.1 0.7 fusion.18
  8.8 0.5 copy-done.8
  9.3 0.9 pad_maximum_fusion.1
  10.2 0.6 gather_fusion.2
  10.8 4.0 collective-permute-start
  14.8 0.7 fusion.19
  16.0 0.6 gather_fusion.3
  16.6 1.3 collective-permute-start.1
  18.5 2.9 reshape.547
  21.4 1.6 collective-permute-done.1
  23.0 0.8 slice_bitcast_fusion
  24.1 1.2 broadcast.582.clone
  25.4 135.9 %while.30 = (s32[]{:T(128)}, f32[96,1664]{0,1:T(8,128)S(1)}, f32[27,96,96]{2,1,0:T(8,128)}, s32[]{:T(128)}, s32[64,128]{1,0:T(8,128)S(1)}, /*index=5*/s32[]{:T(1...) while((s32[]{:T(128)}, f32[96,1664]{0,1:T(8,128)S(1)}, ...), condition=%wide.region_3.4_spmd.clone, body=%wide.region_0.3_spmd.clone.sunk | while | flops 367194624 | bytes 65129680 | solution.py:82
  25.5 0.7 fusion.47
  26.3 2.6 convolution_convert_fusion.4
  28.9 2.6 reshape.676
  31.5 0.6 convolution_bitcast_fusion.8
  32.0 1.8 copy.97
  33.9 3.9 copy.98
  37.7 5.1 copy.99
  42.8 54.4 %scatter_fusion = f32[96,1664]{0,1:T(8,128)S(1)} fusion(f32[96,1664]{0,1:T(8,128)S(1)} %get-tuple-element.624, s32[8192]{0:T(1024)S(1)} %bitcast.203, f32[8192,96]{1,0:T(8,128)} %copy.99), kind=kCustom, calls=%fused_computation.4.clone.clone.1 | custom fusion | flops 786432 | bytes 9469952 | tf_op jit(solution)/shard_map/while/body/scatter-add | solution.py:72
  97.3 24.0 %gather_fusion = bf16[8192,96]{1,0:T(8,128)(2,1)S(1)} fusion(bf16[96,1664]{0,1:T(8,128)(2,1)S(1)} %get-tuple-element.646, s32[8192]{0:T(1024)S(1)} %fusion.48), kind=kCustom, calls=%fused_computation.clone.clone.1 | custom fusion | bytes 3178496 | tf_op jit(solution)/shard_map/while/body/gather | solution.py:56
  121.3 2.6 copy.100
  123.9 2.0 convolution_bitcast_fusion.9
  125.9 2.6 copy.101
  128.5 4.2 broadcast_in_dim.135
  132.8 24.2 %select_reduce_fusion.4 = f32[27,9216]{1,0:T(8,128)} fusion(f32[64,9216]{1,0:T(8,128)} %broadcast_in_dim.135, pred[64,27]{0,1:T(8,128)(4,1)S(1)} %iota_compare_fusion.9), kind=kLoop, calls=%fused_computation.12.clone.1 | loop fusion | flops 31601664 | bytes 3356352 | tf_op jit(solution)/shard_map/while/body/reduce_sum | solution.py:65
  157.0 1.8 reshape.677
  158.8 2.5 add.327
  161.8 1.4 collective-permute-start.2
  163.2 1.3 collective-permute-start.3
  164.5 1.8 reshape.546
  166.7 0.7 scatter_fusion.2
  167.4 2.2 collective-permute-done.3
  169.6 0.7 scatter_fusion.3
  170.4 1.2 broadcast.582
  171.7 135.9 %while.31 = (s32[]{:T(128)}, f32[96,1664]{0,1:T(8,128)S(1)}, f32[27,96,96]{2,1,0:T(8,128)}, s32[]{:T(128)}, s32[64,128]{1,0:T(8,128)S(1)}, /*index=5*/s32[]{:T(1...) while((s32[]{:T(128)}, f32[96,1664]{0,1:T(8,128)S(1)}, ...), condition=%wide.region_9.10_spmd.clone, body=%wide.region_6.9_spmd.clone.sunk | while | flops 367194624 | bytes 65129680 | solution.py:82
  171.7 0.7 fusion.54
  172.5 2.6 convolution_convert_fusion.5
  175.1 2.6 reshape.682
  177.7 0.5 convolution_bitcast_fusion.10
  178.3 1.8 copy.102
  180.1 3.9 copy.103
  184.0 5.1 copy.104
  189.1 54.4 %scatter_fusion.1 = f32[96,1664]{0,1:T(8,128)S(1)} fusion(f32[96,1664]{0,1:T(8,128)S(1)} %get-tuple-element.663, s32[8192]{0:T(1024)S(1)} %bitcast.204, f32[8192,96]{1,0:T(8,128)} %copy.104), kind=kCustom, calls=%fused_computation.5.clone.clone.1 | custom fusion | flops 786432 | bytes 9469952 | tf_op jit(solution)/shard_map/while/body/scatter-add | solution.py:72
  243.5 24.0 %gather_fusion.1 = bf16[8192,96]{1,0:T(8,128)(2,1)S(1)} fusion(bf16[96,1664]{0,1:T(8,128)(2,1)S(1)} %get-tuple-element.685, s32[8192]{0:T(1024)S(1)} %fusion.55), kind=kCustom, calls=%fused_computation.1.clone.clone.1 | custom fusion | bytes 3178496 | tf_op jit(solution)/shard_map/while/body/gather | solution.py:56
  267.6 2.6 copy.105
  270.2 2.0 convolution_bitcast_fusion.11
  272.1 2.6 copy.106
  274.7 4.2 broadcast_in_dim.141
  279.0 24.3 %select_reduce_fusion.5 = f32[27,9216]{1,0:T(8,128)} fusion(f32[64,9216]{1,0:T(8,128)} %broadcast_in_dim.141, pred[64,27]{0,1:T(8,128)(4,1)S(1)} %iota_compare_fusion.11), kind=kLoop, calls=%fused_computation.35.clone.1 | loop fusion | flops 31601664 | bytes 3356352 | tf_op jit(solution)/shard_map/while/body/reduce_sum | solution.py:65
  303.3 1.8 reshape.683
  305.1 2.5 add.337
  308.0 1.3 collective-permute-start.4
  309.3 1.3 collective-permute-start.5
  310.6 1.3 collective-permute-done.4
  311.9 0.7 scatter_fusion.4
  312.6 3.1 collective-permute-done.5
  315.7 0.7 scatter_fusion.5
  316.5 0.7 convert_element_type.21
  317.1 283.2 %all-reduce.5.cloned.1.call-done = (f32[27,96,96]{2,1,0:T(8,128)}, f32[27,96,96]{2,1,0:T(8,128)}) async-done(((f32[27,96,96]{2,1,0:T(8,128)}, f32[27,96,96]{2,1,0:T(8,128)}), (f32[27,96,96]{2,1,0:T(8,128)}, f32[27,96,96]{2,1,0:T(8,128)})) %all-reduce.5.cloned.1.call-update) | async-done | bytes 1990672 | tf_op jit(solution)/shard_map/psum | solution.py:117
  600.3 2.6 copy.136
  602.9 1.1 copy.137
  (59 shorter events, 2.6 us)
Async XLA Ops:
  7.2 15.8 %copy-start.5 = (bf16[4,96,128]{2,1,0:T(8,128)(2,1)S(1)}, bf16[4,96,128]{2,1,0:T(8,128)(2,1)}, u32[]{:S(2)}) copy-start(bf16[4,96,128]{2,1,0:T(8,128)(2,1)} %param.15) | copy-start | bytes 294916
  7.2 593.1 %all-reduce.5.cloned.1.call-start = ((), (), s32[]{:S(2)}) async-start(), calls=%async_computation | async-start | bytes 5308416 | tf_op jit(solution)/shard_map/psum | solution.py:117
  8.8 0.5 copy-start.8
  10.8 10.6 %collective-permute-start = (bf16[4,2,96,128]{3,2,1,0:T(8,128)(2,1)S(1)}, bf16[4,2,96,128]{3,2,1,0:T(8,128)(2,1)S(1)}, u32[]{:S(2)}, u32[]{:S(2)}) collective-permute-start(bf16[4,2,96,128]{3,2,1,0:T(8,128)(2,1)S(1)} %gather_fusion.2), channel_id=1, source_target_pairs={{0,1},{1,2},{2,3},{3,4},{4,5},{5,6},{6,7},{7,8},{8,9},{9,10},{10,1... | collective-permute-start | bytes 589832 | tf_op jit(solution)/shard_map/ppermute | solution.py:15
  15.4 0.5 copy-start.11
  16.6 6.4 %collective-permute-start.1 = (bf16[4,2,96,128]{3,2,1,0:T(8,128)(2,1)S(1)}, bf16[4,2,96,128]{3,2,1,0:T(8,128)(2,1)S(1)}, u32[]{:S(2)}, u32[]{:S(2)}) collective-permute-start(bf16[4,2,96,128]{3,2,1,0:T(8,128)(2,1)S(1)} %gather_fusion.3), channel_id=1, source_target_pairs={{1,0},{2,1},{3,2},{4,3},{5,4},{6,5},{7,6},{8,7},{9,8},{10,9},{11,1... | collective-permute-start | bytes 589832 | tf_op jit(solution)/shard_map/ppermute | solution.py:15
  23.8 1.6 copy-start
  23.8 1.6 copy-start.1
  23.8 1.6 copy-start.7
  23.8 1.6 copy-start.14
  161.4 3.2 copy-start.4
  161.4 4.9 copy-start.3
  161.7 5.0 copy-start.12
  161.7 7.9 %copy-start.9 = (s32[4]{0:T(128)S(1)}, s32[4]{0:T(128)}, u32[]{:S(2)}) copy-start(s32[4]{0:T(128)} %copy-done.8) | copy-start | bytes 52
  161.8 8.6 %copy-start.6 = (bf16[4,96,128]{2,1,0:T(8,128)(2,1)S(1)}, bf16[4,96,128]{2,1,0:T(8,128)(2,1)}, u32[]{:S(2)}) copy-start(bf16[4,96,128]{2,1,0:T(8,128)(2,1)} %param.16) | copy-start | bytes 294916
  161.8 4.9 collective-permute-start.2
  163.2 6.4 %collective-permute-start.3 = (f32[4,96,128]{2,1,0:T(8,128)S(1)}, f32[4,96,128]{2,1,0:T(8,128)S(1)}, u32[]{:S(2)}, u32[]{:S(2)}) collective-permute-start(f32[4,96,128]{2,1,0:T(8,128)S(1)} %get-tuple-element.471), channel_id=1, source_target_pairs={{1,0},{2,1},{3,2},{4,3},{5,4},{6,5},{7,6},{8,7},{9,8},{10,9},{11,1... | collective-permute-start | bytes 589832 | tf_op jit(solution)/shard_map/ppermute | solution.py:15
  307.6 4.3 copy-start.13
  307.6 8.1 %copy-start.10 = (s32[4]{0:T(128)S(1)}, s32[4]{0:T(128)}, u32[]{:S(2)}) copy-start(s32[4]{0:T(128)} %copy-done.8) | copy-start | bytes 52
  308.0 3.9 collective-permute-start.4
  309.3 6.4 %collective-permute-start.5 = (f32[4,96,128]{2,1,0:T(8,128)S(1)}, f32[4,96,128]{2,1,0:T(8,128)S(1)}, u32[]{:S(2)}, u32[]{:S(2)}) collective-permute-start(f32[4,96,128]{2,1,0:T(8,128)S(1)} %get-tuple-element.466), channel_id=1, source_target_pairs={{1,0},{2,1},{3,2},{4,3},{5,4},{6,5},{7,6},{8,7},{9,8},{10,9},{11,1... | collective-permute-start | bytes 589832 | tf_op jit(solution)/shard_map/ppermute | solution.py:15
  600.3 2.6 copy-start.2
Sparse Core Ops, SparseCore 0:
  307.7 292.5 all-reduce.4
where the time goes:
time: 612 us; the launch traced here: 611 us
  waiting for transfers between devices  291 us (48%)
  other arithmetic  171 us (28%)
  local copies, waits for them, and re-layouts  113 us (18%)
  between operations  15 us (2%)
  starting transfers between devices  10.6 us (2%)
  matrix products  10.2 us (2%)
    psum x1, waiting for transfers between devices, body(): grad_one, grad_two = lax.psum((grad_one, grad_two), ('district', 'tile'))  283 us
    scatter-add x2, other arithmetic, step(): dflat.at[:, flat_idx.reshape(-1)]  109 us
    reduce_sum x2, other arithmetic, step(): jnp.sum(jnp.where(onehot[:, :, None], dweight_pairs[:, None, :], 0.0), ax...  48.5 us
    gather x2, local copies, waits for them, and re-layouts, step(): gathered_input_rows = flat_in[:, flat_idx].reshape(chans, out_per, PB, rows)  48 us
  transfers between devices with their start and end apart: 7, of which 5 were waited for; matrix products, arithmetic and copies ran while one was open for 2% of the time, Pallas kernels for 0%

commit v1 on v0

v1 whole, which is shorter than its diff:
```python
import functools

import jax
import jax.numpy as jnp
from jax import lax
from jax.experimental import pallas as pl
from jax.experimental.pallas import tpu as pltpu
from jax.sharding import PartitionSpec as P

K = 27
PB = 16
NB = 4
KB = 4
C = 96
ROW = 128
EXT = NB + 2 * KB
PACKED = 2048
F32 = jnp.float32
BF16 = jnp.bfloat16
VMEM_LIMIT = 32 * 1024 * 1024

SMEM = pl.BlockSpec(memory_space=pltpu.SMEM)
VMEM = pl.BlockSpec(memory_space=pltpu.VMEM)


def remote(src, dst, send_sem, recv_sem, where):
    return pltpu.make_async_remote_copy(
        src_ref=src,
        dst_ref=dst,
        send_sem=send_sem,
        recv_sem=recv_sem,
        device_id=where,
        device_id_type=pl.DeviceIdType.MESH,
    )


def greet(peers):
    barrier = pltpu.get_barrier_semaphore()
    for peer in peers:
        pl.semaphore_signal(barrier, inc=1, device_id=peer, device_id_type=pl.DeviceIdType.MESH)
    pl.semaphore_wait(barrier, len(peers))


def tile_neighbours():
    district = lax.axis_index("district")
    tile = lax.axis_index("tile")
    tiles = lax.axis_size("tile")
    below = (district, lax.rem(tile + tiles - 1, tiles))
    above = (district, lax.rem(tile + 1, tiles))
    has_below = tile > 0
    has_above = tile < tiles - 1
    return below, above, has_below, has_above


def halo_kernel(lo_ref, hi_ref, feat_ref, pre_ref, low_ref, high_ref, out_lo, out_hi, in_lo, in_hi, send, recv):
    below, above, has_below, has_above = tile_neighbours()
    greet((below, above))
    for j in range(KB):
        out_lo[0, j] = feat_ref[lo_ref[0, j]]
        out_lo[1, j] = jnp.maximum(pre_ref[lo_ref[0, j]], 0.0)
        out_hi[0, j] = feat_ref[hi_ref[0, j]]
        out_hi[1, j] = jnp.maximum(pre_ref[hi_ref[0, j]], 0.0)
    up = remote(out_hi, in_lo, send.at[0], recv.at[0], above)
    down = remote(out_lo, in_hi, send.at[1], recv.at[1], below)
    up.start()
    down.start()
    up.wait()
    low_ref[...] = jnp.where(has_below, in_lo[...], jnp.zeros_like(in_lo))
    down.wait()
    high_ref[...] = jnp.where(has_above, in_hi[...], jnp.zeros_like(in_hi))


def halo(send_lo, send_hi, features, pre_act):
    part = jax.ShapeDtypeStruct((2, KB, C, ROW), BF16)
    return pl.pallas_call(
        halo_kernel,
        out_shape=(part, part),
        in_specs=[SMEM, SMEM, VMEM, VMEM],
        out_specs=(VMEM, VMEM),
        scratch_shapes=[pltpu.VMEM((2, KB, C, ROW), BF16)] * 4
        + [pltpu.SemaphoreType.DMA((2,)), pltpu.SemaphoreType.DMA((2,))],
        compiler_params=pltpu.CompilerParams(
            collective_id=0, has_side_effects=True, vmem_limit_bytes=VMEM_LIMIT
        ),
        name="halo",
    )(send_lo, send_hi, features, pre_act)


def give_back_kernel(low_ref, high_ref, lo_ref, hi_ref, in_lo, in_hi, send, recv):
    below, above, has_below, has_above = tile_neighbours()
    greet((below, above))
    up = remote(high_ref, in_lo, send.at[0], recv.at[0], above)
    down = remote(low_ref, in_hi, send.at[1], recv.at[1], below)
    up.start()
    down.start()
    up.wait()
    lo_ref[...] = jnp.where(has_below, in_lo[...], jnp.zeros_like(in_lo))
    down.wait()
    hi_ref[...] = jnp.where(has_above, in_hi[...], jnp.zeros_like(in_hi))


def give_back(low, high):
    part = jax.ShapeDtypeStruct((KB, C, ROW), BF16)
    return pl.pallas_call(
        give_back_kernel,
        out_shape=(part, part),
        in_specs=[VMEM, VMEM],
        out_specs=(VMEM, VMEM),
        scratch_shapes=[pltpu.VMEM((KB, C, ROW), BF16)] * 2
        + [pltpu.SemaphoreType.DMA((2,)), pltpu.SemaphoreType.DMA((2,))],
        compiler_params=pltpu.CompilerParams(
            collective_id=1, has_side_effects=True, vmem_limit_bytes=VMEM_LIMIT
        ),
        name="give_back",
    )(low, high)


def layer_body(count_ref, pin_ref, poff_ref, rmap_ref, w_ref, ext, grad, dwp_ref, own_ref, low_ref, high_ref, dext, dw):
    dext[...] = jnp.zeros_like(dext)
    dw[...] = jnp.zeros_like(dw)
    rows = lax.broadcasted_iota(jnp.int32, (ROW, ROW), 0)

    def block(o, carry):
        maps = rmap_ref[0, pl.ds(pl.multiple_of(o * PB, PB), PB), :]
        g = grad[o]
        for j in range(PB):
            b = pin_ref[0, o * PB + j]
            k = poff_ref[0, o * PB + j]
            picks = jnp.where(rows == maps[j : j + 1, :], 1.0, 0.0).astype(BF16)
            ht = lax.dot_general(picks, g, (((1,), (1,)), ((), ())), preferred_element_type=F32).astype(BF16)
            dw[k, :, 0:C] += jnp.dot(ext[b], ht, preferred_element_type=F32)
            dext[b] += lax.dot_general(w_ref[k], ht, (((1,), (1,)), ((), ())), preferred_element_type=F32)
        return carry

    lax.fori_loop(0, count_ref[0], block, 0)
    own_ref[...] = dext[0:NB]
    low_ref[...] = dext[NB : NB + KB].astype(BF16)
    high_ref[...] = dext[NB + KB :].astype(BF16)
    lane = lax.broadcasted_iota(jnp.int32, (C, ROW), 1)
    for q in range(7):
        a = dw[4 * q]
        b = pltpu.roll(dw[4 * q + 1], 96, 1)
        c = pltpu.roll(dw[4 * q + 2], 64, 1)
        d = pltpu.roll(dw[4 * q + 3], 32, 1)
        base = q * 3 * C
        dwp_ref[base : base + C, :] = jnp.where(lane < 96, a, b)
        dwp_ref[base + C : base + 2 * C, :] = jnp.where(lane < 64, b, c)
        dwp_ref[base + 2 * C : base + 3 * C, :] = jnp.where(lane < 32, c, d)
    dwp_ref[21 * C :, :] = jnp.zeros((PACKED - 21 * C, ROW), F32)


def layer_two_kernel(count_ref, pin_ref, poff_ref, rmap_ref, w_ref, pre_ref, elow_ref, ehigh_ref, grad_ref,
                     dwp_ref, own_ref, low_ref, high_ref, ext, dext, dw):
    ext[0:NB] = jnp.maximum(pre_ref[...], 0.0)
    ext[NB : NB + KB] = elow_ref[1]
    ext[NB + KB :] = ehigh_ref[1]
    layer_body(count_ref, pin_ref, poff_ref, rmap_ref, w_ref, ext, grad_ref, dwp_ref, own_ref, low_ref, high_ref, dext, dw)


def layer_one_kernel(count_ref, pin_ref, poff_ref, rmap_ref, w_ref, feat_ref, elow_ref, ehigh_ref,
                     slo_ref, shi_ref, pre_ref, hown_ref, flo_ref, fhi_ref,
                     dwp_ref, own_ref, low_ref, high_ref, ext, dext, dw, total, grad):
    ext[0:NB] = feat_ref[...]
    ext[NB : NB + KB] = elow_ref[0]
    ext[NB + KB :] = ehigh_ref[0]
    total[...] = hown_ref[...]
    for j in range(KB):
        total[slo_ref[0, j]] += flo_ref[j].astype(F32)
        total[shi_ref[0, j]] += fhi_ref[j].astype(F32)
    grad[...] = jnp.where(pre_ref[...] > 0, total[...], 0.0).astype(BF16)
    layer_body(count_ref, pin_ref, poff_ref, rmap_ref, w_ref, ext, grad, dwp_ref, own_ref, low_ref, high_ref, dext, dw)


LAYER_OUT = (
    jax.ShapeDtypeStruct((PACKED, ROW), F32),
    jax.ShapeDtypeStruct((NB, C, ROW), F32),
    jax.ShapeDtypeStruct((KB, C, ROW), BF16),
    jax.ShapeDtypeStruct((KB, C, ROW), BF16),
)
LAYER_SCRATCH = [
    pltpu.VMEM((EXT, C, ROW), BF16),
    pltpu.VMEM((EXT, C, ROW), F32),
    pltpu.VMEM((K + 1, C, ROW), F32),
]


def layer_two(count, pin, poff, rmap, w, pre_act, low, high, out_grad):
    return pl.pallas_call(
        layer_two_kernel,
        out_shape=LAYER_OUT,
        in_specs=[SMEM] * 3 + [VMEM] * 6,
        out_specs=(VMEM,) * 4,
        scratch_shapes=LAYER_SCRATCH,
        compiler_params=pltpu.CompilerParams(vmem_limit_bytes=VMEM_LIMIT),
        name="layer_two",
    )(count, pin, poff, rmap, w, pre_act, low, high, out_grad)


def layer_one(count, pin, poff, rmap, w, features, low, high, slo, shi, pre_act, hown, flo, fhi):
    return pl.pallas_call(
        layer_one_kernel,
        out_shape=LAYER_OUT,
        in_specs=[SMEM] * 3 + [VMEM] * 5 + [SMEM] * 2 + [VMEM] * 4,
        out_specs=(VMEM,) * 4,
        scratch_shapes=LAYER_SCRATCH + [pltpu.VMEM((NB, C, ROW), F32), pltpu.VMEM((NB, C, ROW), BF16)],
        compiler_params=pltpu.CompilerParams(vmem_limit_bytes=VMEM_LIMIT),
        name="layer_one",
    )(count, pin, poff, rmap, w, features, low, high, slo, shi, pre_act, hown, flo, fhi)


def reduce_kernel(ny, nz, nx, dw1_ref, dw2_ref, low_ref, high_ref, g1_ref, g2_ref, lo_ref, hi_ref,
                  in_lo, in_hi, snd0, rcv0, acc1, snd1, rcv1, acc2, snd2, rcv2, gat3, fin2, fin1,
                  sb, rb, s0, r0, s1, r1, s2, r2, s3, r3, s4, r4, s5, r5, s6, r6):
    half = PACKED // 2
    district = lax.axis_index("district")
    tile = lax.axis_index("tile")
    core = lax.rem(district, 2)
    y = lax.div(district, 2)
    z = lax.div(tile, nx)
    x = lax.rem(tile, nx)
    below, above, has_below, has_above = tile_neighbours()
    other = (district + 1 - 2 * core, tile)
    ys = [lax.rem(y + s, ny) for s in range(1, ny)]
    zs = [lax.rem(z + s, nz) for s in range(1, nz)]
    y_peers = [(i * 2 + core, tile) for i in ys]
    z_peers = [(district, i * nx + x) for i in zs]
    x_peers = [(district, z * nx + lax.rem(x + s, nx)) for s in range(1, nx)]
    along_y = (ny, y, ys, y_peers)
    along_z = (nz, z, zs, z_peers)
    first = (along_y, along_z)
    second = (along_z, along_y)
    outs = (g1_ref, g2_ref)
    dws = (dw1_ref, dw2_ref)

    greet([below, above, other] + y_peers + z_peers + x_peers)

    up = remote(high_ref, in_lo, sb.at[0], rb.at[0], above)
    down = remote(low_ref, in_hi, sb.at[1], rb.at[1], below)

    keep = pl.ds(pl.multiple_of(core * half, half), half)
    away = pl.ds(pl.multiple_of((1 - core) * half, half), half)
    swaps = []
    for g in range(2):
        snd0[g] = dws[g][away, :].astype(BF16)
        swaps.append(remote(snd0.at[g], rcv0.at[g], s0.at[g], r0.at[g], other))
        swaps[g].start()
    up.start()
    down.start()

    stage1 = [[], []]
    for g in range(2):
        n, me, others, peers = first[g]
        part = half // n
        swaps[g].wait()
        acc1[g] = dws[g][keep, :] + rcv0[g].astype(F32)
        snd1[g] = acc1[g].astype(BF16)
        for s in range(n - 1):
            rows = pl.ds(pl.multiple_of(others[s] * part, part), part)
            copy = remote(snd1.at[g, rows, :], rcv1.at[g, s], s1.at[g, s], r1.at[g, s], peers[s])
            copy.start()
            stage1[g].append(copy)

    stage2 = [[], []]
    for g in range(2):
        n, me, others, peers = first[g]
        part = half // n
        total = acc1[g, pl.ds(pl.multiple_of(me * part, part), part), :]
        for s in range(n - 1):
            stage1[g][s].wait()
            total = total + rcv1[g, s].astype(F32)
        acc2[g] = total
        snd2[g] = total.astype(BF16)
        n, me, others, peers = second[g]
        part = part // n
        for s in range(n - 1):
            rows = pl.ds(pl.multiple_of(others[s] * part, part), part)
            copy = remote(snd2.at[g, rows, :], rcv2.at[g, s], s2.at[g, s], r2.at[g, s], peers[s])
            copy.start()
            stage2[g].append(copy)

    stage3 = [[], []]
    for g in range(2):
        n, me, others, peers = second[g]
        part = half // (ny * nz)
        total = acc2[g, pl.ds(pl.multiple_of(me * part, part), part), :]
        for s in range(n - 1):
            stage2[g][s].wait()
            total = total + rcv2[g, s].astype(F32)
        gat3[g, x] = total.astype(BF16)
        for s in range(nx - 1):
            copy = remote(gat3.at[g, x], gat3.at[g, x], s3.at[g, s], r3.at[g, s], x_peers[s])
            copy.start()
            stage3[g].append(copy)

    stage4 = [[], []]
    for g in range(2):
        n, me, others, peers = second[g]
        part = half // (ny * nz)
        for copy in stage3[g]:
            copy.wait()
        total = gat3[g, 0].astype(F32)
        for i in range(1, nx):
            total = total + gat3[g, i].astype(F32)
        rows = pl.ds(pl.multiple_of(me * part, part), part)
        fin2[g, rows, :] = total.astype(BF16)
        for s in range(n - 1):
            copy = remote(fin2.at[g, rows, :], fin2.at[g, rows, :], s4.at[g, s], r4.at[g, s], peers[s])
            copy.start()
            stage4[g].append(copy)

    stage5 = [[], []]
    for g in range(2):
        n, me, others, peers = first[g]
        part = half // n
        for copy in stage4[g]:
            copy.wait()
        rows = pl.ds(pl.multiple_of(me * part, part), part)
        fin1[g, rows, :] = fin2[g]
        for s in range(n - 1):
            copy = remote(fin2.at[g], fin1.at[g, rows, :], s5.at[g, s], r5.at[g, s], peers[s])
            copy.start()
            stage5[g].append(copy)

    up.wait()
    lo_ref[...] = jnp.where(has_below, in_lo[...], jnp.zeros_like(in_lo))
    down.wait()
    hi_ref[...] = jnp.where(has_above, in_hi[...], jnp.zeros_like(in_hi))

    stage6 = []
    for g in range(2):
        for copy in stage5[g]:
            copy.wait()
        copy = remote(fin1.at[g], outs[g].at[keep, :], s6.at[g], r6.at[g], other)
        copy.start()
        stage6.append(copy)
        outs[g][keep, :] = fin1[g]
    for copy in stage6:
        copy.wait()


def reduce_all(ny, nz, nx, dw1, dw2, low, high):
    half = PACKED // 2
    most = max(ny, nz)
    least = min(ny, nz)
    packed = jax.ShapeDtypeStruct((PACKED, ROW), BF16)
    part = jax.ShapeDtypeStruct((KB, C, ROW), BF16)
    last = half // (ny * nz)
    dma = pltpu.SemaphoreType.DMA
    return pl.pallas_call(
        functools.partial(reduce_kernel, ny, nz, nx),
        out_shape=(packed, packed, part, part),
        in_specs=[VMEM] * 4,
        out_specs=(VMEM,) * 4,
        scratch_shapes=[
            pltpu.VMEM((KB, C, ROW), BF16),
            pltpu.VMEM((KB, C, ROW), BF16),
            pltpu.VMEM((2, half, ROW), BF16),
            pltpu.VMEM((2, half, ROW), BF16),
            pltpu.VMEM((2, half, ROW), F32),
            pltpu.VMEM((2, half, ROW), BF16),
            pltpu.VMEM((2, most - 1, half // least, ROW), BF16),
            pltpu.VMEM((2, half // least, ROW), F32),
            pltpu.VMEM((2, half // least, ROW), BF16),
            pltpu.VMEM((2, most - 1, last, ROW), BF16),
            pltpu.VMEM((2, nx, last, ROW), BF16),
            pltpu.VMEM((2, half // least, ROW), BF16),
            pltpu.VMEM((2, half, ROW), BF16),
            dma((2,)), dma((2,)),
            dma((2,)), dma((2,)),
            dma((2, most - 1)), dma((2, most - 1)),
            dma((2, most - 1)), dma((2, most - 1)),
            dma((2, nx - 1)), dma((2, nx - 1)),
            dma((2, most - 1)), dma((2, most - 1)),
            dma((2, most - 1)), dma((2, most - 1)),
            dma((2,)), dma((2,)),
        ],
        compiler_params=pltpu.CompilerParams(
            collective_id=2, has_side_effects=True, vmem_limit_bytes=VMEM_LIMIT
        ),
        name="reduce_all",
    )(dw1, dw2, low, high)


def finish_kernel(slo_ref, shi_ref, own_ref, flo_ref, fhi_ref, g1_ref, g2_ref, fg_ref, w1_ref, w2_ref, total):
    total[...] = own_ref[...]
    for j in range(KB):
        total[slo_ref[0, j]] += flo_ref[j].astype(F32)
        total[shi_ref[0, j]] += fhi_ref[j].astype(F32)
    fg_ref[...] = total[...].astype(BF16)
    lane = lax.broadcasted_iota(jnp.int32, (C, ROW), 1)
    for src, dst in ((g1_ref, w1_ref), (g2_ref, w2_ref)):
        for q in range(7):
            base = q * 3 * C
            r1 = src[base : base + C, :].astype(F32)
            r2 = src[base + C : base + 2 * C, :].astype(F32)
            r3 = src[base + 2 * C : base + 3 * C, :].astype(F32)
            dst[4 * q] = r1[:, 0:C]
            dst[4 * q + 1] = pltpu.roll(jnp.where(lane < 96, r2, r1), 32, 1)[:, 0:C]
            dst[4 * q + 2] = pltpu.roll(jnp.where(lane < 64, r3, r2), 64, 1)[:, 0:C]
            if 4 * q + 3 < K:
                dst[4 * q + 3] = pltpu.roll(r3, 96, 1)[:, 0:C]


def finish(slo, shi, own, flo, fhi, g1, g2):
    kern = jax.ShapeDtypeStruct((K, C, C), F32)
    return pl.pallas_call(
        finish_kernel,
        out_shape=(jax.ShapeDtypeStruct((NB, C, ROW), BF16), kern, kern),
        in_specs=[SMEM] * 2 + [VMEM] * 5,
        out_specs=(VMEM,) * 3,
        scratch_shapes=[pltpu.VMEM((NB, C, ROW), F32)],
        compiler_params=pltpu.CompilerParams(vmem_limit_bytes=VMEM_LIMIT),
        name="finish",
    )(slo, shi, own, flo, fhi, g1, g2)


def body(ny, nz, nx, features, pre_act, out_grad, weight_one, weight_two, block_count, pair_in, pair_off,
         row_map, send_lo, send_hi):
    low, high = halo(send_lo, send_hi, features, pre_act)
    dw2, hown, hlow, hhigh = layer_two(
        block_count, pair_in, pair_off, row_map, weight_two, pre_act, low, high, out_grad
    )
    flo, fhi = give_back(hlow, hhigh)
    dw1, own, dlow, dhigh = layer_one(
        block_count, pair_in, pair_off, row_map, weight_one, features, low, high,
        send_lo, send_hi, pre_act, hown, flo, fhi,
    )
    g1, g2, xlo, xhi = reduce_all(ny, nz, nx, dw1, dw2, dlow, dhigh)
    return finish(send_lo, send_hi, own, xlo, xhi, g1, g2)


def solution(mesh):
    placed = (
        P(("district", "tile"), None, None),
        P(("district", "tile"), None, None),
        P(("district", "tile"), None, None),
        P(),
        P(),
        P(("district", "tile")),
        P(("district", "tile"), None),
        P(("district", "tile"), None),
        P(("district", "tile"), None, None),
        P(("district", "tile"), None),
        P(("district", "tile"), None),
    )
    tiles = mesh.shape["tile"]
    nx = 4 if tiles % 4 == 0 and tiles > 4 else 2
    ny, nz = mesh.shape["district"] // 2, tiles // nx
    return jax.shard_map(
        functools.partial(body, ny, nz, nx),
        mesh=mesh,
        in_specs=placed,
        out_specs=(P(("district", "tile"), None, None), P(), P()),
        check_vma=False,
    )
```

time: 612 us -> 102 us (0.17)
  waiting for transfers between devices: 291 us -> 0 us
  other arithmetic: 171 us -> 0 us
  local copies, waits for them, and re-layouts: 113 us -> 8.05 us
  Pallas kernels: 0 us -> 91.7 us
  between operations: 15 us -> 1.41 us
  starting transfers between devices: 10.6 us -> 0 us
  matrix products: 10.2 us -> 0 us
    psum x1 -> x0, waiting for transfers between devices: 283 us -> none  [body(): grad_one, grad_two = lax.psum((grad_one, grad_two), ('district', 'tile'))]
    scatter-add x6 -> x0, other arithmetic: 112 us -> none  [the longest x2 109 us: step(): dflat.at[:, flat_idx.reshape(-1)]]
    pallas_call x0 -> x6, Pallas kernels: none -> 91.7 us  [the longest x1 54.2 us: reduce_all(): pl.pallas_call(functools.partial(reduce_kernel, ny, nz, nx), out_shape=(p...]
    gather x4 -> x0, local copies, waits for them, and re-layouts: 49.2 us -> none  [the longest x2 48 us: step(): gathered_input_rows = flat_in[:, flat_idx].reshape(chans, out_per, PB, rows)]
    reduce_sum x2 -> x0, other arithmetic: 48.5 us -> none  [step(): jnp.sum(jnp.where(onehot[:, :, None], dweight_pairs[:, None, :], 0.0), ax...]
    reshape x12 -> x0, local copies, waits for them, and re-layouts: 29.4 us -> none  [the longest x2 10.2 us: step(): gathered_grad_rows.reshape(chans, group * rows)]
    ppermute x6 -> x0, starting transfers between devices: 10.6 us -> none  [passed_along(): return lax.ppermute(block, axis, route)]
    dot_general x6 -> x0, matrix products: 10.2 us -> none  [the longest x2 5.2 us: step(): jnp.dot(onehot.astype(jnp.bfloat16), table, preferred_element_type=jnp.fl...]
  transfers between devices with their start and end apart: 7 -> 0, of which waited for: 5 -> 0; matrix products, arithmetic and copies ran while one was open for 2% -> 0% of each run, Pallas kernels for 0% -> 0%
where the time goes in v1:
time: 102 us; the launch traced here: 101 us
  Pallas kernels  91.7 us (90%)
  local copies, waits for them, and re-layouts  8.05 us (8%)
  between operations  1.41 us (1%)
    pallas_call x1, Pallas kernels, reduce_all(): pl.pallas_call(functools.partial(reduce_kernel, ny, nz, nx), out_shape=(p...  54.2 us
    pallas_call x1, Pallas kernels, halo(): pl.pallas_call(halo_kernel, out_shape=(part, part), in_specs=[SMEM, SMEM,...  18.2 us
    pallas_call x1, Pallas kernels, give_back(): pl.pallas_call(give_back_kernel, out_shape=(part, part), in_specs=[VMEM,...  9.58 us
    unnamed x30, local copies, waits for them, and re-layouts  8.05 us
    pallas_call x1, Pallas kernels, layer_one(): pl.pallas_call(layer_one_kernel, out_shape=LAYER_OUT, in_specs=[SMEM] * 3...  3.73 us
    pallas_call x1, Pallas kernels, layer_two(): pl.pallas_call(layer_two_kernel, out_shape=LAYER_OUT, in_specs=[SMEM] * 3...  3.61 us
    pallas_call x1, Pallas kernels, finish(): pl.pallas_call(finish_kernel, out_shape=(jax.ShapeDtypeStruct((NB, C, ROW...  2.35 us

profile of v1, /device:TPU:1, one launch (start us, length us, event | category | flops | bytes accessed | tf_op | source)
XLA Modules:
  0.0 101.1 jit_solution(715452997786368315)
XLA Ops:
  0.6 0.0 copy-start.12
  0.6 0.0 copy-start.10
  1.3 0.0 copy-start
  1.3 0.9 copy-done
  2.2 0.0 copy-start.5
  2.2 0.9 copy-done.5
  3.1 0.0 copy-start.9
  3.1 0.7 copy-done.9
  3.8 0.0 copy-start.11
  3.8 0.7 copy-done.11
  4.4 0.0 copy-start.2
  4.4 0.0 copy-start.6
  4.4 18.2 %halo.1 = (bf16[2,4,96,128]{3,2,1,0:T(8,128)(2,1)S(1)}, bf16[2,4,96,128]{3,2,1,0:T(8,128)(2,1)S(1)}) custom-call(s32[1,4]{1,0:T(1,128)S(1)} %copy-done.9, s32[1,4]{1,0:T(1,128)S(1)} %copy-done.11, bf16[4,96,128]{2,1,0:T(8,128)(2,1)S(1)} %copy-done.5, bf16[4,96,128]{2,1,0:T(8,128)(2,1)S(1)} %copy-done), custom_call_target="tpu_custom_call" | custom-call | tf_op jit(solution)/shard_map/halo/pallas_call | solution.py:75
  22.6 0.0 copy-start.1
  22.7 0.9 copy-done.1
  23.5 0.0 copy-start.3
  23.5 1.1 %copy-done.3 = bf16[27,96,96]{2,1,0:T(8,128)(2,1)S(1)} copy-done((bf16[27,96,96]{2,1,0:T(8,128)(2,1)S(1)}, bf16[27,96,96]{2,1,0:T(8,128)(2,1)}, u32[]{:S(2)}) %copy-start.3) | copy-done | bytes 497688
  24.6 0.0 copy-start.7
  24.6 0.8 copy-done.7
  25.4 0.0 copy-start.8
  25.4 0.9 copy-done.8
  26.3 0.0 copy-start.13
  26.3 0.7 copy-done.13
  26.9 0.0 copy-start.14
  26.9 0.7 copy-done.14
  27.6 0.0 copy-start.4
  27.6 3.6 %layer_two.1 = (f32[2048,128]{1,0:T(8,128)S(1)}, f32[4,96,128]{2,1,0:T(8,128)S(1)}, bf16[4,96,128]{2,1,0:T(8,128)(2,1)S(1)}, bf16[4,96,128]{2,1,0:T(8,128)(2,1)S(1)}) custom-call(s32[1]{0:T(128)S(6)} %copy.14.count_ref, s32[1,64]{1,0:T(1,128)S(1)} %copy-done.13, s32[1,64]{1,0:T(1,128)S(1)} %copy-done.14, s32[1,64,128]{2,1,0:T(8,128)S(1)} %copy-done.7, ...), custom_call_target="tpu_custom_call" | custom-call | tf_op jit(solution)/shard_map/layer_two/pallas_call | solution.py:188
  31.2 9.6 %give_back.1 = (bf16[4,96,128]{2,1,0:T(8,128)(2,1)S(1)}, bf16[4,96,128]{2,1,0:T(8,128)(2,1)S(1)}) custom-call(bf16[4,96,128]{2,1,0:T(8,128)(2,1)S(1)} %get-tuple-element.22.low_ref, bf16[4,96,128]{2,1,0:T(8,128)(2,1)S(1)} %get-tuple-element.23.high_ref), custom_call_target="tpu_custom_call" | custom-call | tf_op jit(solution)/shard_map/give_back/pallas_call | solution.py:104
  40.8 0.0 copy-done.12
  40.8 0.0 copy-done.10
  40.8 0.0 copy-done.2
  40.8 0.0 copy-done.6
  40.8 0.0 copy-done.4
  40.8 3.7 %layer_one.1 = (f32[2048,128]{1,0:T(8,128)S(1)}, f32[4,96,128]{2,1,0:T(8,128)S(1)}, bf16[4,96,128]{2,1,0:T(8,128)(2,1)S(1)}, bf16[4,96,128]{2,1,0:T(8,128)(2,1)S(1)}) custom-call(s32[1]{0:T(128)S(6)} %copy.14.count_ref, s32[1,64]{1,0:T(1,128)S(1)} %copy-done.13, s32[1,64]{1,0:T(1,128)S(1)} %copy-done.14, s32[1,64,128]{2,1,0:T(8,128)S(1)} %copy-done.7, ...), custom_call_target="tpu_custom_call" | custom-call | tf_op jit(solution)/shard_map/layer_one/pallas_call | solution.py:200
  44.6 54.2 %reduce_all.1 = (bf16[2048,128]{1,0:T(8,128)(2,1)S(1)}, bf16[2048,128]{1,0:T(8,128)(2,1)S(1)}, bf16[4,96,128]{2,1,0:T(8,128)(2,1)S(1)}, bf16[4,96,128]{2,1,0:T(8,128)(2,1)S(1)}) custom-call(f32[2048,128]{1,0:T(8,128)S(1)} %get-tuple-element.27.dw1_ref, f32[2048,128]{1,0:T(8,128)S(1)} %get-tuple-element.28.dw2_ref, ...), custom_call_target="tpu_custom_call" | custom-call | tf_op jit(solution)/shard_map/reduce_all/pallas_call | solution.py:349
  98.8 2.3 %finish.1 = (bf16[4,96,128]{2,1,0:T(8,128)(2,1)}, f32[27,96,96]{2,1,0:T(8,128)}, f32[27,96,96]{2,1,0:T(8,128)}) custom-call(s32[1,4]{1,0:T(1,128)S(1)} %copy-done.10, s32[1,4]{1,0:T(1,128)S(1)} %copy-done.12, f32[4,96,128]{2,1,0:T(8,128)S(1)} %get-tuple-element.26.own_ref, bf16[4,96,128]{2,1,0:T(8,128)(2,1)S(1)} %get-tuple-element.31.flo_ref, ...), custom_call_target="tpu_custom_call" | custom-call | tf_op jit(solution)/shard_map/finish/pallas_call | solution.py:406
Async XLA Ops:
  0.6 40.2 %copy-start.12 = (s32[1,4]{1,0:T(1,128)S(1)}, s32[1,4]{1,0:T(1,128)}, u32[]{:S(2)}) copy-start(s32[1,4]{1,0:T(1,128)} %shi_ref.3) | copy-start | bytes 52
  0.6 40.2 %copy-start.10 = (s32[1,4]{1,0:T(1,128)S(1)}, s32[1,4]{1,0:T(1,128)}, u32[]{:S(2)}) copy-start(s32[1,4]{1,0:T(1,128)} %slo_ref.3) | copy-start | bytes 52
  1.3 0.9 copy-start
  2.2 0.9 copy-start.5
  3.1 0.7 copy-start.9
  3.8 0.7 copy-start.11
  4.4 36.4 %copy-start.2 = (bf16[4,96,128]{2,1,0:T(8,128)(2,1)S(1)}, bf16[4,96,128]{2,1,0:T(8,128)(2,1)}, u32[]{:S(2)}) copy-start(bf16[4,96,128]{2,1,0:T(8,128)(2,1)} %pre_ref.5) | copy-start | bytes 294916
  4.4 36.4 %copy-start.6 = (bf16[4,96,128]{2,1,0:T(8,128)(2,1)S(1)}, bf16[4,96,128]{2,1,0:T(8,128)(2,1)}, u32[]{:S(2)}) copy-start(bf16[4,96,128]{2,1,0:T(8,128)(2,1)} %feat_ref.3) | copy-start | bytes 294916
  22.6 0.9 copy-start.1
  23.5 1.1 %copy-start.3 = (bf16[27,96,96]{2,1,0:T(8,128)(2,1)S(1)}, bf16[27,96,96]{2,1,0:T(8,128)(2,1)}, u32[]{:S(2)}) copy-start(bf16[27,96,96]{2,1,0:T(8,128)(2,1)} %w_ref.2) | copy-start | bytes 1492996
  24.6 0.8 copy-start.7
  25.4 0.9 copy-start.8
  26.3 0.7 copy-start.13
  26.9 0.7 copy-start.14
  27.6 13.2 %copy-start.4 = (bf16[27,96,96]{2,1,0:T(8,128)(2,1)S(1)}, bf16[27,96,96]{2,1,0:T(8,128)(2,1)}, u32[]{:S(2)}) copy-start(bf16[27,96,96]{2,1,0:T(8,128)(2,1)} %w_ref.3) | copy-start | bytes 1492996

commit v2 on v0

v2 whole, which is shorter than its diff:
```python
import functools

import jax
import jax.numpy as jnp
from jax import lax
from jax.experimental import pallas as pl
from jax.experimental.pallas import tpu as pltpu
from jax.sharding import PartitionSpec as P

K = 27
PB = 16
NB = 4
KB = 4
C = 96
ROW = 128
EXT = NB + 2 * KB
PAIRS = NB * PB
UNROLL = 32
NT = (((1,), (1,)), ((), ()))
PACKED = 2048
F32 = jnp.float32
BF16 = jnp.bfloat16
VMEM_LIMIT = 56 * 1024 * 1024

HBM = pl.BlockSpec(memory_space=pltpu.HBM)
SMEM = pl.BlockSpec(memory_space=pltpu.SMEM)
VMEM = pl.BlockSpec(memory_space=pltpu.VMEM)


def remote(src, dst, send_sem, recv_sem, where):
    return pltpu.make_async_remote_copy(
        src_ref=src,
        dst_ref=dst,
        send_sem=send_sem,
        recv_sem=recv_sem,
        device_id=where,
        device_id_type=pl.DeviceIdType.MESH,
    )


def tile_neighbours():
    district = lax.axis_index("district")
    tile = lax.axis_index("tile")
    tiles = lax.axis_size("tile")
    below = (district, lax.rem(tile + tiles - 1, tiles))
    above = (district, lax.rem(tile + 1, tiles))
    has_below = tile > 0
    has_above = tile < tiles - 1
    return below, above, has_below, has_above


def sort_pairs(keys, table, row):
    p = lax.broadcasted_iota(jnp.int32, (PAIRS, PAIRS), 0)
    q = lax.broadcasted_iota(jnp.int32, (PAIRS, PAIRS), 1)
    column = jnp.sum(jnp.where(p == q, keys, 0), axis=1, keepdims=True)
    ahead = jnp.logical_or(keys < column, jnp.logical_and(keys == column, q < p))
    rank = jnp.sum(jnp.where(ahead, 1, 0), axis=1, keepdims=True)
    table[row : row + 1, 0:PAIRS] = jnp.sum(jnp.where(rank == q, p, 0), axis=0, keepdims=True)
    lane = lax.broadcasted_iota(jnp.int32, (PAIRS, ROW), 1)
    table[row + 1 : row + 2, :] = jnp.sum(jnp.where(column <= lane, 1, 0), axis=0, keepdims=True)
    table[row + 2 : row + 3, :] = jnp.sum(jnp.where(column < lane, 1, 0), axis=0, keepdims=True)


def build_picks(rmap, count, picks):
    rows = lax.broadcasted_iota(jnp.int32, (ROW, ROW), 0)

    def block(o, carry):
        maps = rmap[0, pl.ds(pl.multiple_of(o * PB, PB), PB), :] + jnp.where(o < count, 0, 2 * ROW)
        for j in range(PB):
            picks[o * PB + j] = jnp.where(rows == maps[j : j + 1, :], 1.0, 0.0).astype(BF16)
        return carry

    lax.fori_loop(0, NB, block, 0)


def scatter_grads(picks, gt, ht):
    def step(i, carry):
        for j in range(UNROLL):
            product = jnp.dot(picks[i * UNROLL + j], gt[i * (UNROLL // PB) + j // PB], preferred_element_type=F32)
            ht[i * UNROLL + j] = product.astype(BF16)
        return carry

    lax.fori_loop(0, PAIRS // UNROLL, step, 0)


def running_sums(product, row, keys, table, sums):
    def step(i, carry):
        total, before = carry
        for j in range(UNROLL):
            at = i * UNROLL + j
            p = table[row, at]
            key = keys[0, p]
            total = total * jnp.where(key == before, 1.0, 0.0) + product(p)
            sums[at] = total
            before = key
        return total, before

    lax.fori_loop(0, PAIRS // UNROLL, step, (jnp.zeros((C, ROW), F32), jnp.int32(-1)))


def sum_of(key, row, table, sums):
    upto = table[row + 1, key]
    some = jnp.where(upto > table[row + 2, key], 1.0, 0.0)
    return sums[jnp.maximum(upto - 1, 0)] * some


def pack(table, sums, packed):
    lane = lax.broadcasted_iota(jnp.int32, (C, ROW), 1)

    def group(q, carry):
        a = sum_of(4 * q, 0, table, sums)
        b = pltpu.roll(sum_of(4 * q + 1, 0, table, sums), 96, 1)
        c = pltpu.roll(sum_of(4 * q + 2, 0, table, sums), 64, 1)
        d = pltpu.roll(sum_of(4 * q + 3, 0, table, sums), 32, 1)
        base = pl.multiple_of(q * 3 * C, 3 * C)
        packed[pl.ds(base, C), :] = jnp.where(lane < 96, a, b)
        packed[pl.ds(base + C, C), :] = jnp.where(lane < 64, b, c)
        packed[pl.ds(base + 2 * C, C), :] = jnp.where(lane < 32, c, d)
        return carry

    lax.fori_loop(0, 7, group, 0)
    packed[21 * C :, :] = jnp.zeros((PACKED - 21 * C, ROW), F32)


def fused_kernel(ny, nz, nx, *refs):
    (feat_in, pre_in, og_in, w1_in, w2_in, count_in, pin_in, poff_in, rmap_in, slo_in, shi_in,
     g1_ref, g2_ref, own_ref, xlo_ref, xhi_ref,
     feat, pre, og, w1, w2, rmap, pin_v, poff_v, count, pin, poff, slo, shi, table_v, table,
     picks, gt, ht, sums, ext_h, ext_x, own2,
     out_lo, out_hi, in_lo, in_hi, gb_lo, gb_hi, fb_lo, fb_hi, gb2_lo, gb2_hi,
     dwp, rcv0, snd1, rcv1, mine, gat3, fin1,
     load, tsem, hs, hr, gs, gr, g2s, g2r, s0, r0, s1, r1, s3, r3, s5, r5, s6, r6) = refs
    half = PACKED // 2
    part = half // (ny * nx)
    district = lax.axis_index("district")
    tile = lax.axis_index("tile")
    core = lax.rem(district, 2)
    y = lax.div(district, 2)
    z = lax.div(tile, nx)
    x = lax.rem(tile, nx)
    below, above, has_below, has_above = tile_neighbours()
    other = (district + 1 - 2 * core, tile)

    def reach(step):
        return -min(step[0], ny - step[0]) - min(step[1], nx - step[1])

    steps = sorted([(a, b) for a in range(ny) for b in range(nx) if a + b], key=reach)
    plane = [(lax.rem(y + a, ny), lax.rem(x + b, nx)) for a, b in steps]
    plane_peers = [(i * 2 + core, z * nx + j) for i, j in plane]
    z_order = sorted(range(1, nz), key=lambda a: -min(a, nz - a))
    z_peers = [(district, lax.rem(z + a, nz) * nx + x) for a in z_order]

    loads = {}
    pieces = (("rmap", rmap_in, rmap), ("count", count_in, count), ("poff_v", poff_in, poff_v), ("pin_v", pin_in, pin_v),
              ("og", og_in, og), ("pin", pin_in, pin), ("poff", poff_in, poff), ("slo", slo_in, slo), ("shi", shi_in, shi),
              ("pre", pre_in, pre), ("feat", feat_in, feat), ("w2", w2_in, w2), ("w1", w1_in, w1))
    for i, (name, src, dst) in enumerate(pieces):
        loads[name] = pltpu.make_async_copy(src, dst, load.at[i])
        loads[name].start()
    barrier = pltpu.get_barrier_semaphore()
    peers = plane_peers + z_peers + [other, below, above]
    for peer in peers:
        pl.semaphore_signal(barrier, inc=1, device_id=peer, device_id_type=pl.DeviceIdType.MESH)

    gt[...] = jnp.zeros_like(gt)
    table_v[...] = jnp.zeros_like(table_v)
    loads["poff_v"].wait()
    loads["pin_v"].wait()
    sort_pairs(poff_v[...], table_v, 0)
    sort_pairs(pin_v[...], table_v, 3)
    to_scalar = pltpu.make_async_copy(table_v, table, tsem)
    to_scalar.start()
    loads["rmap"].wait()
    loads["count"].wait()
    build_picks(rmap, count[0], picks)
    loads["og"].wait()
    for b in range(NB):
        gt[b, :, 0:C] = jnp.transpose(og[b])
    scatter_grads(picks, gt, ht)

    for name in ("slo", "shi", "pre", "feat"):
        loads[name].wait()
    for j in range(KB):
        out_lo[0, j] = jnp.maximum(pre[slo[0, j]], 0.0)
        out_hi[0, j] = jnp.maximum(pre[shi[0, j]], 0.0)
        out_lo[1, j] = feat[slo[0, j]]
        out_hi[1, j] = feat[shi[0, j]]
    pl.semaphore_wait(barrier, len(peers))
    halo = []
    for f in range(2):
        halo.append((
            remote(out_hi.at[f], in_lo.at[f], hs.at[0, f], hr.at[0, f], above),
            remote(out_lo.at[f], in_hi.at[f], hs.at[1, f], hr.at[1, f], below),
        ))
    for copy in halo[0]:
        copy.start()

    for name in ("pin", "poff", "w2"):
        loads[name].wait()
    to_scalar.wait()
    running_sums(
        lambda p: lax.dot_general(w2[poff[0, p]], ht[p, :, 0:C], NT, preferred_element_type=F32),
        3, pin, table, sums,
    )
    for j in range(KB):
        gb_lo[j] = sum_of(NB + j, 3, table, sums).astype(gb_lo.dtype)
        gb_hi[j] = sum_of(NB + KB + j, 3, table, sums).astype(gb_hi.dtype)
    back = (
        remote(gb_hi, fb_lo, gs.at[0], gr.at[0], above),
        remote(gb_lo, fb_hi, gs.at[1], gr.at[1], below),
    )
    for copy in back:
        copy.start()
    for copy in halo[1]:
        copy.start()
    for b in range(NB):
        own2[b] = sum_of(b, 3, table, sums)

    def extend(f, own, ext):
        ext[0:NB] = own
        halo[f][0].wait()
        ext[NB : NB + KB] = jnp.where(has_below, in_lo[f], jnp.zeros_like(in_lo[f]))
        halo[f][1].wait()
        ext[NB + KB :] = jnp.where(has_above, in_hi[f], jnp.zeros_like(in_hi[f]))

    def weight_sums(ext):
        running_sums(
            lambda p: jnp.dot(ext[pin[0, p]], ht[p], preferred_element_type=F32), 0, poff, table, sums
        )

    keep = pl.ds(pl.multiple_of(core * half, half), half)
    away = pl.ds(pl.multiple_of((1 - core) * half, half), half)
    chunk = pl.ds(pl.multiple_of((y * nx + x) * part, part), part)
    outs = (g1_ref, g2_ref)

    def swap_halves(g):
        copy = remote(dwp.at[g, away, :], rcv0.at[g], s0.at[g], r0.at[g], other)
        copy.start()
        return [copy]

    def scatter_plane(g, waits):
        for copy in waits:
            copy.wait()
        snd1[g] = (dwp[g, keep, :] + rcv0[g]).astype(BF16)
        copies = []
        for s in range(len(plane)):
            i, j = plane[s]
            rows = pl.ds(pl.multiple_of((i * nx + j) * part, part), part)
            copies.append(remote(snd1.at[g, rows, :], rcv1.at[g, s], s1.at[g, s], r1.at[g, s], plane_peers[s]))
            copies[s].start()
        at = pl.ds(pl.multiple_of(core * half + (y * nx + x) * part, part), part)
        mine[g] = dwp[g, at, :] + rcv0[g, chunk, :]
        return copies

    def exchange_z(g, waits):
        for copy in waits:
            copy.wait()
        total = mine[g]
        for s in range(len(plane)):
            total = total + rcv1[g, s].astype(F32)
        gat3[g, z] = total.astype(BF16)
        copies = []
        for s in range(nz - 1):
            copies.append(remote(gat3.at[g, z], gat3.at[g, z], s3.at[g, s], r3.at[g, s], z_peers[s]))
            copies[s].start()
        return copies

    def gather_plane(g, waits):
        for copy in waits:
            copy.wait()
        total = gat3[g, 0].astype(F32)
        for i in range(1, nz):
            total = total + gat3[g, i].astype(F32)
        fin1[g, chunk, :] = total.astype(BF16)
        copies = []
        for s in range(len(plane)):
            copies.append(remote(fin1.at[g, chunk, :], fin1.at[g, chunk, :], s5.at[g, s], r5.at[g, s], plane_peers[s]))
            copies[s].start()
        return copies

    def share_halves(g, waits):
        for copy in waits:
            copy.wait()
        copy = remote(fin1.at[g], outs[g].at[keep, :], s6.at[g], r6.at[g], other)
        copy.start()
        outs[g][keep, :] = fin1[g]
        return [copy]

    extend(0, jnp.maximum(pre[...], 0.0), ext_h)
    weight_sums(ext_h)
    pack(table, sums, dwp.at[1])
    two = swap_halves(1)
    two = scatter_plane(1, two)

    for copy in back:
        copy.wait()
    for b in range(NB):
        total = own2[b]
        for j in range(KB):
            from_below = jnp.where(jnp.logical_and(slo[0, j] == b, has_below), 1.0, 0.0)
            from_above = jnp.where(jnp.logical_and(shi[0, j] == b, has_above), 1.0, 0.0)
            total = total + from_below * fb_lo[j].astype(F32) + from_above * fb_hi[j].astype(F32)
        gt[b, :, 0:C] = jnp.transpose(jnp.where(pre[b] > 0, total, 0.0).astype(BF16))
    scatter_grads(picks, gt, ht)
    extend(1, feat[...], ext_x)
    weight_sums(ext_x)
    pack(table, sums, dwp.at[0])
    one = swap_halves(0)
    two = exchange_z(1, two)
    one = scatter_plane(0, one)

    loads["w1"].wait()
    running_sums(
        lambda p: lax.dot_general(w1[poff[0, p]], ht[p, :, 0:C], NT, preferred_element_type=F32),
        3, pin, table, sums,
    )
    for j in range(KB):
        gb2_lo[j] = sum_of(NB + j, 3, table, sums)
        gb2_hi[j] = sum_of(NB + KB + j, 3, table, sums)
    for b in range(NB):
        own_ref[b] = sum_of(b, 3, table, sums)

    one = exchange_z(0, one)
    last = (
        remote(gb2_hi, xlo_ref, g2s.at[0], g2r.at[0], above),
        remote(gb2_lo, xhi_ref, g2s.at[1], g2r.at[1], below),
    )
    for copy in last:
        copy.start()
    two = gather_plane(1, two)
    one = gather_plane(0, one)
    two = share_halves(1, two)
    one = share_halves(0, one)
    for copy in list(last) + two + one:
        copy.wait()


def fused(ny, nz, nx, *operands):
    half = PACKED // 2
    part = half // (ny * nx)
    near = ny * nx - 1
    dma = pltpu.SemaphoreType.DMA
    packed = jax.ShapeDtypeStruct((PACKED, ROW), BF16)
    blocks = jax.ShapeDtypeStruct((NB, C, ROW), F32)
    four = pltpu.VMEM((NB, C, ROW), BF16)
    four_wide = pltpu.VMEM((NB, C, ROW), F32)
    kernel_weights = pltpu.VMEM((K, C, C), BF16)
    return pl.pallas_call(
        functools.partial(fused_kernel, ny, nz, nx),
        out_shape=(packed, packed, blocks, blocks, blocks),
        in_specs=[HBM] * 11,
        out_specs=(VMEM,) * 5,
        scratch_shapes=[
            four, four, four, kernel_weights, kernel_weights,
            pltpu.VMEM((1, PAIRS, ROW), jnp.int32),
            pltpu.VMEM((1, PAIRS), jnp.int32),
            pltpu.VMEM((1, PAIRS), jnp.int32),
            pltpu.SMEM((1,), jnp.int32),
            pltpu.SMEM((1, PAIRS), jnp.int32),
            pltpu.SMEM((1, PAIRS), jnp.int32),
            pltpu.SMEM((1, KB), jnp.int32),
            pltpu.SMEM((1, KB), jnp.int32),
            pltpu.VMEM((8, ROW), jnp.int32),
            pltpu.SMEM((8, ROW), jnp.int32),
            pltpu.VMEM((PAIRS, ROW, ROW), BF16),
            pltpu.VMEM((NB, ROW, ROW), BF16),
            pltpu.VMEM((PAIRS, ROW, ROW), BF16),
            pltpu.VMEM((PAIRS, C, ROW), F32),
            pltpu.VMEM((EXT, C, ROW), BF16),
            pltpu.VMEM((EXT, C, ROW), BF16),
            four_wide,
            pltpu.VMEM((2, KB, C, ROW), BF16),
            pltpu.VMEM((2, KB, C, ROW), BF16),
            pltpu.VMEM((2, KB, C, ROW), BF16),
            pltpu.VMEM((2, KB, C, ROW), BF16),
            four, four, four, four, four_wide, four_wide,
            pltpu.VMEM((2, PACKED, ROW), F32),
            pltpu.VMEM((2, half, ROW), F32),
            pltpu.VMEM((2, half, ROW), BF16),
            pltpu.VMEM((2, near, part, ROW), BF16),
            pltpu.VMEM((2, part, ROW), F32),
            pltpu.VMEM((2, nz, part, ROW), BF16),
            pltpu.VMEM((2, half, ROW), BF16),
            dma((13,)), dma,
            dma((2, 2)), dma((2, 2)),
            dma((2,)), dma((2,)),
            dma((2,)), dma((2,)),
            dma((2,)), dma((2,)),
            dma((2, near)), dma((2, near)),
            dma((2, nz - 1)), dma((2, nz - 1)),
            dma((2, near)), dma((2, near)),
            dma((2,)), dma((2,)),
        ],
        compiler_params=pltpu.CompilerParams(
            collective_id=0, has_side_effects=True, vmem_limit_bytes=VMEM_LIMIT
        ),
        name="fused",
    )(*operands)


def finish_kernel(slo_ref, shi_ref, own_ref, flo_ref, fhi_ref, g1_ref, g2_ref, fg_ref, w1_ref, w2_ref, total):
    below, above, has_below, has_above = tile_neighbours()
    total[...] = own_ref[...]
    for j in range(KB):
        total[slo_ref[0, j]] += flo_ref[j] * jnp.where(has_below, 1.0, 0.0)
        total[shi_ref[0, j]] += fhi_ref[j] * jnp.where(has_above, 1.0, 0.0)
    fg_ref[...] = total[...].astype(BF16)
    lane = lax.broadcasted_iota(jnp.int32, (C, ROW), 1)
    for src, dst in ((g1_ref, w1_ref), (g2_ref, w2_ref)):
        for q in range(7):
            base = q * 3 * C
            r1 = src[base : base + C, :].astype(F32)
            r2 = src[base + C : base + 2 * C, :].astype(F32)
            r3 = src[base + 2 * C : base + 3 * C, :].astype(F32)
            dst[4 * q] = r1[:, 0:C]
            dst[4 * q + 1] = pltpu.roll(jnp.where(lane < 96, r2, r1), 32, 1)[:, 0:C]
            dst[4 * q + 2] = pltpu.roll(jnp.where(lane < 64, r3, r2), 64, 1)[:, 0:C]
            if 4 * q + 3 < K:
                dst[4 * q + 3] = pltpu.roll(r3, 96, 1)[:, 0:C]


def finish(slo, shi, own, flo, fhi, g1, g2):
    kern = jax.ShapeDtypeStruct((K, C, C), F32)
    return pl.pallas_call(
        finish_kernel,
        out_shape=(jax.ShapeDtypeStruct((NB, C, ROW), BF16), kern, kern),
        in_specs=[SMEM] * 2 + [VMEM] * 5,
        out_specs=(VMEM,) * 3,
        scratch_shapes=[pltpu.VMEM((NB, C, ROW), F32)],
        compiler_params=pltpu.CompilerParams(vmem_limit_bytes=VMEM_LIMIT),
        name="finish",
    )(slo, shi, own, flo, fhi, g1, g2)


def body(ny, nz, nx, features, pre_act, out_grad, weight_one, weight_two, block_count, pair_in, pair_off,
         row_map, send_lo, send_hi):
    g1, g2, own, xlo, xhi = fused(
        ny, nz, nx, features, pre_act, out_grad, weight_one, weight_two, block_count, pair_in, pair_off,
        row_map, send_lo, send_hi,
    )
    return finish(send_lo, send_hi, own, xlo, xhi, g1, g2)


def solution(mesh):
    placed = (
        P(("district", "tile"), None, None),
        P(("district", "tile"), None, None),
        P(("district", "tile"), None, None),
        P(),
        P(),
        P(("district", "tile")),
        P(("district", "tile"), None),
        P(("district", "tile"), None),
        P(("district", "tile"), None, None),
        P(("district", "tile"), None),
        P(("district", "tile"), None),
    )
    tiles = mesh.shape["tile"]
    nx = 4 if tiles % 4 == 0 and tiles > 4 else 2
    ny, nz = mesh.shape["district"] // 2, tiles // nx
    return jax.shard_map(
        functools.partial(body, ny, nz, nx),
        mesh=mesh,
        in_specs=placed,
        out_specs=(P(("district", "tile"), None, None), P(), P()),
        check_vma=False,
    )
```

time: 612 us -> 67 us (0.11)
  waiting for transfers between devices: 291 us -> 0 us
  other arithmetic: 171 us -> 0 us
  local copies, waits for them, and re-layouts: 113 us -> 0 us
  Pallas kernels: 0 us -> 65.6 us
  between operations: 15 us -> 1.29 us
  starting transfers between devices: 10.6 us -> 0 us
  matrix products: 10.2 us -> 0 us
    psum x1 -> x0, waiting for transfers between devices: 283 us -> none  [body(): grad_one, grad_two = lax.psum((grad_one, grad_two), ('district', 'tile'))]
    scatter-add x6 -> x0, other arithmetic: 112 us -> none  [the longest x2 109 us: step(): dflat.at[:, flat_idx.reshape(-1)]]
    pallas_call x0 -> x2, Pallas kernels: none -> 65.6 us  [the longest x1 62.4 us: fused(): pl.pallas_call(functools.partial(fused_kernel, ny, nz, nx), out_shape=(pa...]
    gather x4 -> x0, local copies, waits for them, and re-layouts: 49.2 us -> none  [the longest x2 48 us: step(): gathered_input_rows = flat_in[:, flat_idx].reshape(chans, out_per, PB, rows)]
    reduce_sum x2 -> x0, other arithmetic: 48.5 us -> none  [step(): jnp.sum(jnp.where(onehot[:, :, None], dweight_pairs[:, None, :], 0.0), ax...]
    reshape x12 -> x0, local copies, waits for them, and re-layouts: 29.4 us -> none  [the longest x2 10.2 us: step(): gathered_grad_rows.reshape(chans, group * rows)]
    ppermute x6 -> x0, starting transfers between devices: 10.6 us -> none  [passed_along(): return lax.ppermute(block, axis, route)]
    dot_general x6 -> x0, matrix products: 10.2 us -> none  [the longest x2 5.2 us: step(): jnp.dot(onehot.astype(jnp.bfloat16), table, preferred_element_type=jnp.fl...]
  transfers between devices with their start and end apart: 7 -> 0, of which waited for: 5 -> 0; matrix products, arithmetic and copies ran while one was open for 2% -> 0% of each run, Pallas kernels for 0% -> 0%
where the time goes in v2:
time: 67 us; the launch traced here: 66.9 us
  Pallas kernels  65.6 us (98%)
  between operations  1.29 us (2%)
    pallas_call x1, Pallas kernels, fused(): pl.pallas_call(functools.partial(fused_kernel, ny, nz, nx), out_shape=(pa...  62.4 us
    pallas_call x1, Pallas kernels, finish(): pl.pallas_call(finish_kernel, out_shape=(jax.ShapeDtypeStruct((NB, C, ROW...  3.19 us

profile of v2, /device:TPU:1, one launch (start us, length us, event | category | flops | bytes accessed | tf_op | source)
XLA Modules:
  0.0 66.9 jit_solution(12390107835212620810)
XLA Ops:
  1.3 62.4 %fused.1 = (bf16[2048,128]{1,0:T(8,128)(2,1)}, bf16[2048,128]{1,0:T(8,128)(2,1)}, f32[4,96,128]{2,1,0:T(8,128)}, f32[4,96,128]{2,1,0:T(8,128)}, f32[4,96,128]{2,1,0:T(8,128)}) custom-call(bf16[4,96,128]{2,1,0:T(8,128)(2,1)} %refs_0_.1, bf16[4,96,128]{2,1,0:T(8,128)(2,1)} %refs_1_.1, bf16[4,96,128]{2,1,0:T(8,128)(2,1)} %refs_2_.1, ...), custom_call_target="tpu_custom_call" | custom-call | tf_op jit(solution)/shard_map/fused/pallas_call | solution.py:348
  63.7 3.2 %finish.1 = (bf16[4,96,128]{2,1,0:T(8,128)(2,1)}, f32[27,96,96]{2,1,0:T(8,128)}, f32[27,96,96]{2,1,0:T(8,128)}) custom-call(s32[1,4]{1,0:T(1,128)} %slo_ref.1, s32[1,4]{1,0:T(1,128)} %shi_ref.1, f32[4,96,128]{2,1,0:T(8,128)} %get-tuple-element.8.own_ref, f32[4,96,128]{2,1,0:T(8,128)} %get-tuple-element.9.flo_ref, f32[4,96,128]{2,1,0:T(8,128)} %get-tuple-element.10.fhi_ref, ...), custom_call_target="tpu_custom_call" | custom-call | tf_op jit(solution)/shard_map/finish/pallas_call | solution.py:424

commit v3 on v2

--- a/solution.py
+++ b/solution.py
@@ -20,7 +20,7 @@
 PACKED = 2048
 F32 = jnp.float32
 BF16 = jnp.bfloat16
-VMEM_LIMIT = 56 * 1024 * 1024
+VMEM_LIMIT = 24 * 1024 * 1024
 
 HBM = pl.BlockSpec(memory_space=pltpu.HBM)
 SMEM = pl.BlockSpec(memory_space=pltpu.SMEM)
@@ -78,6 +78,16 @@
         for j in range(UNROLL):
             product = jnp.dot(picks[i * UNROLL + j], gt[i * (UNROLL // PB) + j // PB], preferred_element_type=F32)
             ht[i * UNROLL + j] = product.astype(BF16)
+        return carry
+
+    lax.fori_loop(0, PAIRS // UNROLL, step, 0)
+
+
+def gather_rows(picks, pin, ext, gathered):
+    def step(i, carry):
+        for j in range(UNROLL):
+            p = i * UNROLL + j
+            gathered[p] = jnp.dot(ext[pin[0, p]], picks[p], preferred_element_type=F32).astype(BF16)
         return carry
 
     lax.fori_loop(0, PAIRS // UNROLL, step, 0)
@@ -126,7 +136,7 @@
     (feat_in, pre_in, og_in, w1_in, w2_in, count_in, pin_in, poff_in, rmap_in, slo_in, shi_in,
      g1_ref, g2_ref, own_ref, xlo_ref, xhi_ref,
      feat, pre, og, w1, w2, rmap, pin_v, poff_v, count, pin, poff, slo, shi, table_v, table,
-     picks, gt, ht, sums, ext_h, ext_x, own2,
+     picks, gt, ht, gathered, sums, ext_h, ext_x, own2,
      out_lo, out_hi, in_lo, in_hi, gb_lo, gb_hi, fb_lo, fb_hi, gb2_lo, gb2_hi,
      dwp, rcv0, snd1, rcv1, mine, gat3, fin1,
      load, tsem, hs, hr, gs, gr, g2s, g2r, s0, r0, s1, r1, s3, r3, s5, r5, s6, r6) = refs
@@ -223,11 +233,6 @@
         halo[f][1].wait()
         ext[NB + KB :] = jnp.where(has_above, in_hi[f], jnp.zeros_like(in_hi[f]))
 
-    def weight_sums(ext):
-        running_sums(
-            lambda p: jnp.dot(ext[pin[0, p]], ht[p], preferred_element_type=F32), 0, poff, table, sums
-        )
-
     keep = pl.ds(pl.multiple_of(core * half, half), half)
     away = pl.ds(pl.multiple_of((1 - core) * half, half), half)
     chunk = pl.ds(pl.multiple_of((y * nx + x) * part, part), part)
@@ -287,9 +292,13 @@
         return [copy]
 
     extend(0, jnp.maximum(pre[...], 0.0), ext_h)
-    weight_sums(ext_h)
+    running_sums(
+        lambda p: jnp.dot(ext_h[pin[0, p]], ht[p], preferred_element_type=F32), 0, poff, table, sums
+    )
     pack(table, sums, dwp.at[1])
     two = swap_halves(1)
+    extend(1, feat[...], ext_x)
+    gather_rows(picks, pin, ext_x, gathered)
     two = scatter_plane(1, two)
 
     for copy in back:
@@ -301,13 +310,14 @@
             from_above = jnp.where(jnp.logical_and(shi[0, j] == b, has_above), 1.0, 0.0)
             total = total + from_below * fb_lo[j].astype(F32) + from_above * fb_hi[j].astype(F32)
         gt[b, :, 0:C] = jnp.transpose(jnp.where(pre[b] > 0, total, 0.0).astype(BF16))
-    scatter_grads(picks, gt, ht)
-    extend(1, feat[...], ext_x)
-    weight_sums(ext_x)
+    running_sums(
+        lambda p: jnp.dot(gathered[p], gt[p // PB], preferred_element_type=F32), 0, poff, table, sums
+    )
     pack(table, sums, dwp.at[0])
     one = swap_halves(0)
+    scatter_grads(picks, gt, ht)
+    one = scatter_plane(0, one)
     two = exchange_z(1, two)
-    one = scatter_plane(0, one)
 
     loads["w1"].wait()
     running_sums(
@@ -321,13 +331,13 @@
         own_ref[b] = sum_of(b, 3, table, sums)
 
     one = exchange_z(0, one)
+    two = gather_plane(1, two)
     last = (
         remote(gb2_hi, xlo_ref, g2s.at[0], g2r.at[0], above),
         remote(gb2_lo, xhi_ref, g2s.at[1], g2r.at[1], below),
     )
     for copy in last:
         copy.start()
-    two = gather_plane(1, two)
     one = gather_plane(0, one)
     two = share_halves(1, two)
     one = share_halves(0, one)
@@ -365,6 +375,7 @@
             pltpu.VMEM((PAIRS, ROW, ROW), BF16),
             pltpu.VMEM((NB, ROW, ROW), BF16),
             pltpu.VMEM((PAIRS, ROW, ROW), BF16),
+            pltpu.VMEM((PAIRS, C, ROW), BF16),
             pltpu.VMEM((PAIRS, C, ROW), F32),
             pltpu.VMEM((EXT, C, ROW), BF16),
             pltpu.VMEM((EXT, C, ROW), BF16),
@@ -398,25 +409,37 @@
     )(*operands)
 
 
-def finish_kernel(slo_ref, shi_ref, own_ref, flo_ref, fhi_ref, g1_ref, g2_ref, fg_ref, w1_ref, w2_ref, total):
+def finish_kernel(slo_ref, shi_ref, own_ref, flo_ref, fhi_ref, g1_ref, g2_ref, fg_ref, w1_ref, w2_ref,
+                  total, rounded, wide, sems, last):
+    lane = lax.broadcasted_iota(jnp.int32, (C, ROW), 1)
+    copies = []
+    for g, (src, dst) in enumerate(((g1_ref, w1_ref), (g2_ref, w2_ref))):
+        for q in range(7):
+            base = q * 3 * C
+            size = min(4, K - 4 * q)
+            r1 = src[base : base + C, :].astype(F32)
+            r2 = src[base + C : base + 2 * C, :].astype(F32)
+            r3 = src[base + 2 * C : base + 3 * C, :].astype(F32)
+            wide[g, 4 * q] = r1[:, 0:C]
+            wide[g, 4 * q + 1] = pltpu.roll(jnp.where(lane < 96, r2, r1), 32, 1)[:, 0:C]
+            wide[g, 4 * q + 2] = pltpu.roll(jnp.where(lane < 64, r3, r2), 64, 1)[:, 0:C]
+            if size == 4:
+                wide[g, 4 * q + 3] = pltpu.roll(r3, 96, 1)[:, 0:C]
+            copy = pltpu.make_async_copy(
+                wide.at[g, pl.ds(4 * q, size)], dst.at[pl.ds(4 * q, size)], sems.at[g, q]
+            )
+            copy.start()
+            copies.append(copy)
     below, above, has_below, has_above = tile_neighbours()
     total[...] = own_ref[...]
     for j in range(KB):
         total[slo_ref[0, j]] += flo_ref[j] * jnp.where(has_below, 1.0, 0.0)
         total[shi_ref[0, j]] += fhi_ref[j] * jnp.where(has_above, 1.0, 0.0)
-    fg_ref[...] = total[...].astype(BF16)
-    lane = lax.broadcasted_iota(jnp.int32, (C, ROW), 1)
-    for src, dst in ((g1_ref, w1_ref), (g2_ref, w2_ref)):
-        for q in range(7):
-            base = q * 3 * C
-            r1 = src[base : base + C, :].astype(F32)
-            r2 = src[base + C : base + 2 * C, :].astype(F32)
-            r3 = src[base + 2 * C : base + 3 * C, :].astype(F32)
-            dst[4 * q] = r1[:, 0:C]
-            dst[4 * q + 1] = pltpu.roll(jnp.where(lane < 96, r2, r1), 32, 1)[:, 0:C]
-            dst[4 * q + 2] = pltpu.roll(jnp.where(lane < 64, r3, r2), 64, 1)[:, 0:C]
-            if 4 * q + 3 < K:
-                dst[4 * q + 3] = pltpu.roll(r3, 96, 1)[:, 0:C]
+    rounded[...] = total[...].astype(BF16)
+    copy = pltpu.make_async_copy(rounded, fg_ref, last)
+    copy.start()
+    for copy in copies + [copy]:
+        copy.wait()
 
 
 def finish(slo, shi, own, flo, fhi, g1, g2):
@@ -425,8 +448,14 @@
         finish_kernel,
         out_shape=(jax.ShapeDtypeStruct((NB, C, ROW), BF16), kern, kern),
         in_specs=[SMEM] * 2 + [VMEM] * 5,
-        out_specs=(VMEM,) * 3,
-        scratch_shapes=[pltpu.VMEM((NB, C, ROW), F32)],
+        out_specs=(HBM,) * 3,
+        scratch_shapes=[
+            pltpu.VMEM((NB, C, ROW), F32),
+            pltpu.VMEM((NB, C, ROW), BF16),
+            pltpu.VMEM((2, K, C, C), F32),
+            pltpu.SemaphoreType.DMA((2, 7)),
+            pltpu.SemaphoreType.DMA,
+        ],
         compiler_params=pltpu.CompilerParams(vmem_limit_bytes=VMEM_LIMIT),
         name="finish",
     )(slo, shi, own, flo, fhi, g1, g2)
@@ -434,10 +463,10 @@
 
 def body(ny, nz, nx, features, pre_act, out_grad, weight_one, weight_two, block_count, pair_in, pair_off,
          row_map, send_lo, send_hi):
-    g1, g2, own, xlo, xhi = fused(
-        ny, nz, nx, features, pre_act, out_grad, weight_one, weight_two, block_count, pair_in, pair_off,
-        row_map, send_lo, send_hi,
-    )
+    operands = (features, pre_act, out_grad, weight_one, weight_two, block_count, pair_in, pair_off,
+                row_map, send_lo, send_hi)
+    operands = [a if a.shape == (1,) else pltpu.with_memory_space_constraint(a, pltpu.HBM) for a in operands]
+    g1, g2, own, xlo, xhi = fused(ny, nz, nx, *operands)
     return finish(send_lo, send_hi, own, xlo, xhi, g1, g2)
 
 

time: 67 us -> 63.2 us (0.943)
  Pallas kernels: 65.6 us -> 61.7 us
    pallas_call x1, Pallas kernels: 62.4 us -> 59.4 us  [fused(): pl.pallas_call(functools.partial(fused_kernel, ny, nz, nx), out_shape=(pa...]
    pallas_call x1, Pallas kernels: 3.19 us -> 2.28 us  [finish(): pl.pallas_call(finish_kernel, out_shape=(jax.ShapeDtypeStruct((NB, C, ROW...]
where the time goes in v3:
time: 63.2 us; the launch traced here: 63.1 us
  Pallas kernels  61.7 us (98%)
  between operations  1.34 us (2%)
    pallas_call x1, Pallas kernels, fused(): pl.pallas_call(functools.partial(fused_kernel, ny, nz, nx), out_shape=(pa...  59.4 us
    pallas_call x1, Pallas kernels, finish(): pl.pallas_call(finish_kernel, out_shape=(jax.ShapeDtypeStruct((NB, C, ROW...  2.28 us

profile of v3, /device:TPU:1, one launch (start us, length us, event | category | flops | bytes accessed | tf_op | source)
XLA Modules:
  0.0 63.1 jit_solution(11624548805183078158)
XLA Ops:
  0.6 0.0 copy-start.1
  0.6 0.0 copy-start
  1.3 59.4 %fused.1 = (bf16[2048,128]{1,0:T(8,128)(2,1)S(1)}, bf16[2048,128]{1,0:T(8,128)(2,1)S(1)}, f32[4,96,128]{2,1,0:T(8,128)S(1)}, f32[4,96,128]{2,1,0:T(8,128)S(1)}, f32[4,96,128]{2,1,0:T(8,128)S(1)}) custom-call(bf16[4,96,128]{2,1,0:T(8,128)(2,1)} %refs_0_.1, bf16[4,96,128]{2,1,0:T(8,128)(2,1)} %refs_1_.1, bf16[4,96,128]{2,1,0:T(8,128)(2,1)} %refs_2_.1, ...), custom_call_target="tpu_custom_call" | custom-call | tf_op jit(solution)/shard_map/fused/pallas_call | solution.py:358
  60.8 0.0 copy-done.1
  60.8 0.0 copy-done
  60.8 2.3 %finish.1 = (bf16[4,96,128]{2,1,0:T(8,128)(2,1)}, f32[27,96,96]{2,1,0:T(8,128)}, f32[27,96,96]{2,1,0:T(8,128)}) custom-call(s32[1,4]{1,0:T(1,128)S(1)} %copy-done, s32[1,4]{1,0:T(1,128)S(1)} %copy-done.1, f32[4,96,128]{2,1,0:T(8,128)S(1)} %get-tuple-element.8.own_ref, f32[4,96,128]{2,1,0:T(8,128)S(1)} %get-tuple-element.9.flo_ref, ...), custom_call_target="tpu_custom_call" | custom-call | tf_op jit(solution)/shard_map/finish/pallas_call | solution.py:447
Async XLA Ops:
  0.6 60.1 %copy-start.1 = (s32[1,4]{1,0:T(1,128)S(1)}, s32[1,4]{1,0:T(1,128)}, u32[]{:S(2)}) copy-start(s32[1,4]{1,0:T(1,128)} %shi_ref.1) | copy-start | bytes 52
  0.6 60.1 %copy-start = (s32[1,4]{1,0:T(1,128)S(1)}, s32[1,4]{1,0:T(1,128)}, u32[]{:S(2)}) copy-start(s32[1,4]{1,0:T(1,128)} %slo_ref.1) | copy-start | bytes 52

commit v4 on v3

--- a/solution.py
+++ b/solution.py
@@ -23,7 +23,6 @@
 VMEM_LIMIT = 24 * 1024 * 1024
 
 HBM = pl.BlockSpec(memory_space=pltpu.HBM)
-SMEM = pl.BlockSpec(memory_space=pltpu.SMEM)
 VMEM = pl.BlockSpec(memory_space=pltpu.VMEM)
 
 
@@ -36,6 +35,10 @@
         device_id=where,
         device_id_type=pl.DeviceIdType.MESH,
     )
+
+
+def wait_all(like, sem):
+    pltpu.make_async_copy(like, like, sem).wait()
 
 
 def tile_neighbours():
@@ -134,14 +137,13 @@
 
 def fused_kernel(ny, nz, nx, *refs):
     (feat_in, pre_in, og_in, w1_in, w2_in, count_in, pin_in, poff_in, rmap_in, slo_in, shi_in,
-     g1_ref, g2_ref, own_ref, xlo_ref, xhi_ref,
+     g1_ref, g2_ref, fg_ref,
      feat, pre, og, w1, w2, rmap, pin_v, poff_v, count, pin, poff, slo, shi, table_v, table,
-     picks, gt, ht, gathered, sums, ext_h, ext_x, own2,
-     out_lo, out_hi, in_lo, in_hi, gb_lo, gb_hi, fb_lo, fb_hi, gb2_lo, gb2_hi,
+     picks, gt, ht, gathered, sums, ext_h, ext_x, own,
+     out_lo, out_hi, in_lo, in_hi, gb_lo, gb_hi, fb_lo, fb_hi, gb2_lo, gb2_hi, fb2_lo, fb2_hi,
      dwp, rcv0, snd1, rcv1, mine, gat3, fin1,
      load, tsem, hs, hr, gs, gr, g2s, g2r, s0, r0, s1, r1, s3, r3, s5, r5, s6, r6) = refs
     half = PACKED // 2
-    part = half // (ny * nx)
     district = lax.axis_index("district")
     tile = lax.axis_index("tile")
     core = lax.rem(district, 2)
@@ -151,14 +153,30 @@
     below, above, has_below, has_above = tile_neighbours()
     other = (district + 1 - 2 * core, tile)
 
-    def reach(step):
-        return -min(step[0], ny - step[0]) - min(step[1], nx - step[1])
-
-    steps = sorted([(a, b) for a in range(ny) for b in range(nx) if a + b], key=reach)
-    plane = [(lax.rem(y + a, ny), lax.rem(x + b, nx)) for a, b in steps]
-    plane_peers = [(i * 2 + core, z * nx + j) for i, j in plane]
-    z_order = sorted(range(1, nz), key=lambda a: -min(a, nz - a))
-    z_peers = [(district, lax.rem(z + a, nz) * nx + x) for a in z_order]
+    def plane_of(n, me, device):
+        steps = sorted(
+            [(a, b) for a in range(n) for b in range(nx) if a + b],
+            key=lambda step: -min(step[0], n - step[0]) - min(step[1], nx - step[1]),
+        )
+        places = [(lax.rem(me + a, n), lax.rem(x + b, nx)) for a, b in steps]
+        return [i * nx + j for i, j in places], [device(i, j) for i, j in places]
+
+    def line_of(n, me, device):
+        order = sorted(range(1, n), key=lambda a: -min(a, n - a))
+        return [device(lax.rem(me + a, n), x) for a in order]
+
+    def over_y(i, j):
+        return (i * 2 + core, z * nx + j)
+
+    def over_z(i, j):
+        return (district, i * nx + j)
+
+    planes = (plane_of(ny, y, over_y), plane_of(nz, z, over_z))
+    lines = (line_of(nz, z, over_z), line_of(ny, y, over_y))
+    own_part = (y * nx + x, z * nx + x)
+    own_slot = (z, y)
+    parts = (half // (ny * nx), half // (nz * nx))
+    slots = (nz, ny)
 
     loads = {}
     pieces = (("rmap", rmap_in, rmap), ("count", count_in, count), ("poff_v", poff_in, poff_v), ("pin_v", pin_in, pin_v),
@@ -168,7 +186,8 @@
         loads[name] = pltpu.make_async_copy(src, dst, load.at[i])
         loads[name].start()
     barrier = pltpu.get_barrier_semaphore()
-    peers = plane_peers + z_peers + [other, below, above]
+    peers = planes[0][1] + [other, below, above]
+    peers += [over_z(lax.rem(z + a, nz), lax.rem(x + b, nx)) for a in range(1, nz) for b in range(nx)]
     for peer in peers:
         pl.semaphore_signal(barrier, inc=1, device_id=peer, device_id_type=pl.DeviceIdType.MESH)
 
@@ -182,7 +201,7 @@
     to_scalar.start()
     loads["rmap"].wait()
     loads["count"].wait()
-    build_picks(rmap, count[0], picks)
+    build_picks(rmap, count[0, 0], picks)
     loads["og"].wait()
     for b in range(NB):
         gt[b, :, 0:C] = jnp.transpose(og[b])
@@ -195,6 +214,18 @@
         out_hi[0, j] = jnp.maximum(pre[shi[0, j]], 0.0)
         out_lo[1, j] = feat[slo[0, j]]
         out_hi[1, j] = feat[shi[0, j]]
+    for name in ("pin", "poff", "w2"):
+        loads[name].wait()
+    to_scalar.wait()
+    running_sums(
+        lambda p: lax.dot_general(w2[poff[0, p]], ht[p, :, 0:C], NT, preferred_element_type=F32),
+        3, pin, table, sums,
+    )
+    for j in range(KB):
+        gb_lo[j] = sum_of(NB + j, 3, table, sums).astype(gb_lo.dtype)
+        gb_hi[j] = sum_of(NB + KB + j, 3, table, sums).astype(gb_hi.dtype)
+    for b in range(NB):
+        own[b] = sum_of(b, 3, table, sums)
     pl.semaphore_wait(barrier, len(peers))
     halo = []
     for f in range(2):
@@ -202,29 +233,12 @@
             remote(out_hi.at[f], in_lo.at[f], hs.at[0, f], hr.at[0, f], above),
             remote(out_lo.at[f], in_hi.at[f], hs.at[1, f], hr.at[1, f], below),
         ))
-    for copy in halo[0]:
-        copy.start()
-
-    for name in ("pin", "poff", "w2"):
-        loads[name].wait()
-    to_scalar.wait()
-    running_sums(
-        lambda p: lax.dot_general(w2[poff[0, p]], ht[p, :, 0:C], NT, preferred_element_type=F32),
-        3, pin, table, sums,
-    )
-    for j in range(KB):
-        gb_lo[j] = sum_of(NB + j, 3, table, sums).astype(gb_lo.dtype)
-        gb_hi[j] = sum_of(NB + KB + j, 3, table, sums).astype(gb_hi.dtype)
     back = (
         remote(gb_hi, fb_lo, gs.at[0], gr.at[0], above),
         remote(gb_lo, fb_hi, gs.at[1], gr.at[1], below),
     )
-    for copy in back:
+    for copy in list(halo[1]) + list(back) + list(halo[0]):
         copy.start()
-    for copy in halo[1]:
-        copy.start()
-    for b in range(NB):
-        own2[b] = sum_of(b, 3, table, sums)
 
     def extend(f, own, ext):
         ext[0:NB] = own
@@ -235,90 +249,88 @@
 
     keep = pl.ds(pl.multiple_of(core * half, half), half)
     away = pl.ds(pl.multiple_of((1 - core) * half, half), half)
-    chunk = pl.ds(pl.multiple_of((y * nx + x) * part, part), part)
+    chunks = [pl.ds(pl.multiple_of(own_part[g] * parts[g], parts[g]), parts[g]) for g in range(2)]
     outs = (g1_ref, g2_ref)
 
     def swap_halves(g):
-        copy = remote(dwp.at[g, away, :], rcv0.at[g], s0.at[g], r0.at[g], other)
-        copy.start()
-        return [copy]
-
-    def scatter_plane(g, waits):
-        for copy in waits:
-            copy.wait()
+        remote(dwp.at[g, away, :], rcv0.at[g], s0.at[g], r0.at[g], other).start()
+
+    def scatter_plane(g):
+        wait_all(rcv0.at[g], r0.at[g])
         snd1[g] = (dwp[g, keep, :] + rcv0[g]).astype(BF16)
-        copies = []
-        for s in range(len(plane)):
-            i, j = plane[s]
-            rows = pl.ds(pl.multiple_of((i * nx + j) * part, part), part)
-            copies.append(remote(snd1.at[g, rows, :], rcv1.at[g, s], s1.at[g, s], r1.at[g, s], plane_peers[s]))
-            copies[s].start()
-        at = pl.ds(pl.multiple_of(core * half + (y * nx + x) * part, part), part)
-        mine[g] = dwp[g, at, :] + rcv0[g, chunk, :]
-        return copies
-
-    def exchange_z(g, waits):
-        for copy in waits:
-            copy.wait()
-        total = mine[g]
-        for s in range(len(plane)):
-            total = total + rcv1[g, s].astype(F32)
-        gat3[g, z] = total.astype(BF16)
-        copies = []
-        for s in range(nz - 1):
-            copies.append(remote(gat3.at[g, z], gat3.at[g, z], s3.at[g, s], r3.at[g, s], z_peers[s]))
-            copies[s].start()
-        return copies
-
-    def gather_plane(g, waits):
-        for copy in waits:
-            copy.wait()
-        total = gat3[g, 0].astype(F32)
-        for i in range(1, nz):
-            total = total + gat3[g, i].astype(F32)
-        fin1[g, chunk, :] = total.astype(BF16)
-        copies = []
-        for s in range(len(plane)):
-            copies.append(remote(fin1.at[g, chunk, :], fin1.at[g, chunk, :], s5.at[g, s], r5.at[g, s], plane_peers[s]))
-            copies[s].start()
-        return copies
-
-    def share_halves(g, waits):
-        for copy in waits:
-            copy.wait()
-        copy = remote(fin1.at[g], outs[g].at[keep, :], s6.at[g], r6.at[g], other)
-        copy.start()
+        part = parts[g]
+        for s, (index, peer) in enumerate(zip(*planes[g])):
+            rows = pl.ds(pl.multiple_of(index * part, part), part)
+            remote(snd1.at[g, rows, :], rcv1.at[g, s, 0:part], s1.at[g], r1.at[g], peer).start()
+        at = pl.ds(pl.multiple_of(core * half + own_part[g] * part, part), part)
+        mine[g, 0:part] = dwp[g, at, :] + rcv0[g, chunks[g], :]
+
+    def exchange_line(g):
+        part = parts[g]
+        near = half // part - 1
+        wait_all(rcv1.at[g, 0:near, 0:part], r1.at[g])
+        total = mine[g, 0:part]
+        for s in range(near):
+            total = total + rcv1[g, s, 0:part].astype(F32)
+        gat3[g, own_slot[g], 0:part] = total.astype(BF16)
+        for peer in lines[g]:
+            block = gat3.at[g, own_slot[g], 0:part]
+            remote(block, block, s3.at[g], r3.at[g], peer).start()
+
+    def gather_plane(g):
+        part = parts[g]
+        wait_all(gat3.at[g, 0 : slots[g] - 1, 0:part], r3.at[g])
+        total = gat3[g, 0, 0:part].astype(F32)
+        for i in range(1, slots[g]):
+            total = total + gat3[g, i, 0:part].astype(F32)
+        fin1[g, chunks[g], :] = total.astype(BF16)
+        block = fin1.at[g, chunks[g], :]
+        for peer in planes[g][1]:
+            remote(block, block, s5.at[g], r5.at[g], peer).start()
+
+    def share_halves(g):
+        wait_all(fin1.at[g, 0 : half - parts[g]], r5.at[g])
+        remote(fin1.at[g], outs[g].at[keep, :], s6.at[g], r6.at[g], other).start()
         outs[g][keep, :] = fin1[g]
-        return [copy]
+
+    def settle(g):
+        wait_all(rcv0.at[g], s0.at[g])
+        wait_all(snd1.at[g, 0 : half - parts[g]], s1.at[g])
+        wait_all(gat3.at[g, 0 : slots[g] - 1, 0 : parts[g]], s3.at[g])
+        wait_all(fin1.at[g, 0 : half - parts[g]], s5.at[g])
+        wait_all(fin1.at[g], s6.at[g])
+        wait_all(fin1.at[g], r6.at[g])
+
+    def add_back(b, total, lo, hi):
+        for j in range(KB):
+            from_below = jnp.where(jnp.logical_and(slo[0, j] == b, has_below), 1.0, 0.0)
+            from_above = jnp.where(jnp.logical_and(shi[0, j] == b, has_above), 1.0, 0.0)
+            total = total + from_below * lo[j].astype(F32) + from_above * hi[j].astype(F32)
+        return total
+
+    extend(1, feat[...], ext_x)
+    gather_rows(picks, pin, ext_x, gathered)
+    for copy in back:
+        copy.wait()
+    for b in range(NB):
+        hidden_grad = add_back(b, own[b], fb_lo, fb_hi)
+        gt[b, :, 0:C] = jnp.transpose(jnp.where(pre[b] > 0, hidden_grad, 0.0).astype(BF16))
+    running_sums(
+        lambda p: jnp.dot(gathered[p], gt[p // PB], preferred_element_type=F32), 0, poff, table, sums
+    )
+    pack(table, sums, dwp.at[0])
+    swap_halves(0)
 
     extend(0, jnp.maximum(pre[...], 0.0), ext_h)
     running_sums(
         lambda p: jnp.dot(ext_h[pin[0, p]], ht[p], preferred_element_type=F32), 0, poff, table, sums
     )
     pack(table, sums, dwp.at[1])
-    two = swap_halves(1)
-    extend(1, feat[...], ext_x)
-    gather_rows(picks, pin, ext_x, gathered)
-    two = scatter_plane(1, two)
-
-    for copy in back:
-        copy.wait()
-    for b in range(NB):
-        total = own2[b]
-        for j in range(KB):
-            from_below = jnp.where(jnp.logical_and(slo[0, j] == b, has_below), 1.0, 0.0)
-            from_above = jnp.where(jnp.logical_and(shi[0, j] == b, has_above), 1.0, 0.0)
-            total = total + from_below * fb_lo[j].astype(F32) + from_above * fb_hi[j].astype(F32)
-        gt[b, :, 0:C] = jnp.transpose(jnp.where(pre[b] > 0, total, 0.0).astype(BF16))
-    running_sums(
-        lambda p: jnp.dot(gathered[p], gt[p // PB], preferred_element_type=F32), 0, poff, table, sums
-    )
-    pack(table, sums, dwp.at[0])
-    one = swap_halves(0)
+    swap_halves(1)
+    scatter_plane(0)
+    scatter_plane(1)
+
     scatter_grads(picks, gt, ht)
-    one = scatter_plane(0, one)
-    two = exchange_z(1, two)
-
     loads["w1"].wait()
     running_sums(
         lambda p: lax.dot_general(w1[poff[0, p]], ht[p, :, 0:C], NT, preferred_element_type=F32),
@@ -328,44 +340,50 @@
         gb2_lo[j] = sum_of(NB + j, 3, table, sums)
         gb2_hi[j] = sum_of(NB + KB + j, 3, table, sums)
     for b in range(NB):
-        own_ref[b] = sum_of(b, 3, table, sums)
-
-    one = exchange_z(0, one)
-    two = gather_plane(1, two)
+        own[b] = sum_of(b, 3, table, sums)
+
+    exchange_line(0)
+    exchange_line(1)
     last = (
-        remote(gb2_hi, xlo_ref, g2s.at[0], g2r.at[0], above),
-        remote(gb2_lo, xhi_ref, g2s.at[1], g2r.at[1], below),
+        remote(gb2_hi, fb2_lo, g2s.at[0], g2r.at[0], above),
+        remote(gb2_lo, fb2_hi, g2s.at[1], g2r.at[1], below),
     )
     for copy in last:
         copy.start()
-    one = gather_plane(0, one)
-    two = share_halves(1, two)
-    one = share_halves(0, one)
-    for copy in list(last) + two + one:
+    gather_plane(0)
+    gather_plane(1)
+    for copy in last:
         copy.wait()
+    for b in range(NB):
+        fg_ref[b] = add_back(b, own[b], fb2_lo, fb2_hi).astype(BF16)
+    share_halves(0)
+    share_halves(1)
+    settle(0)
+    settle(1)
 
 
 def fused(ny, nz, nx, *operands):
     half = PACKED // 2
-    part = half // (ny * nx)
-    near = ny * nx - 1
+    part = half // (min(ny, nz) * nx)
+    most = max(ny, nz)
+    near = most * nx - 1
     dma = pltpu.SemaphoreType.DMA
     packed = jax.ShapeDtypeStruct((PACKED, ROW), BF16)
-    blocks = jax.ShapeDtypeStruct((NB, C, ROW), F32)
+    blocks = jax.ShapeDtypeStruct((NB, C, ROW), BF16)
     four = pltpu.VMEM((NB, C, ROW), BF16)
     four_wide = pltpu.VMEM((NB, C, ROW), F32)
     kernel_weights = pltpu.VMEM((K, C, C), BF16)
     return pl.pallas_call(
         functools.partial(fused_kernel, ny, nz, nx),
-        out_shape=(packed, packed, blocks, blocks, blocks),
+        out_shape=(packed, packed, blocks),
         in_specs=[HBM] * 11,
-        out_specs=(VMEM,) * 5,
+        out_specs=(VMEM,) * 3,
         scratch_shapes=[
             four, four, four, kernel_weights, kernel_weights,
             pltpu.VMEM((1, PAIRS, ROW), jnp.int32),
             pltpu.VMEM((1, PAIRS), jnp.int32),
             pltpu.VMEM((1, PAIRS), jnp.int32),
-            pltpu.SMEM((1,), jnp.int32),
+            pltpu.SMEM((1, 1), jnp.int32),
             pltpu.SMEM((1, PAIRS), jnp.int32),
             pltpu.SMEM((1, PAIRS), jnp.int32),
             pltpu.SMEM((1, KB), jnp.int32),
@@ -384,22 +402,22 @@
             pltpu.VMEM((2, KB, C, ROW), BF16),
             pltpu.VMEM((2, KB, C, ROW), BF16),
             pltpu.VMEM((2, KB, C, ROW), BF16),
-            four, four, four, four, four_wide, four_wide,
+            four, four, four, four, four_wide, four_wide, four_wide, four_wide,
             pltpu.VMEM((2, PACKED, ROW), F32),
             pltpu.VMEM((2, half, ROW), F32),
             pltpu.VMEM((2, half, ROW), BF16),
             pltpu.VMEM((2, near, part, ROW), BF16),
             pltpu.VMEM((2, part, ROW), F32),
-            pltpu.VMEM((2, nz, part, ROW), BF16),
+            pltpu.VMEM((2, most, part, ROW), BF16),
             pltpu.VMEM((2, half, ROW), BF16),
             dma((13,)), dma,
             dma((2, 2)), dma((2, 2)),
             dma((2,)), dma((2,)),
             dma((2,)), dma((2,)),
             dma((2,)), dma((2,)),
-            dma((2, near)), dma((2, near)),
-            dma((2, nz - 1)), dma((2, nz - 1)),
-            dma((2, near)), dma((2, near)),
+            dma((2,)), dma((2,)),
+            dma((2,)), dma((2,)),
+            dma((2,)), dma((2,)),
             dma((2,)), dma((2,)),
         ],
         compiler_params=pltpu.CompilerParams(
@@ -409,10 +427,11 @@
     )(*operands)
 
 
-def finish_kernel(slo_ref, shi_ref, own_ref, flo_ref, fhi_ref, g1_ref, g2_ref, fg_ref, w1_ref, w2_ref,
-                  total, rounded, wide, sems, last):
+def finish_kernel(grad_ref, g1_ref, g2_ref, fg_ref, w1_ref, w2_ref, wide, sems, last):
     lane = lax.broadcasted_iota(jnp.int32, (C, ROW), 1)
-    copies = []
+    first = pltpu.make_async_copy(grad_ref, fg_ref, last)
+    first.start()
+    copies = [first]
     for g, (src, dst) in enumerate(((g1_ref, w1_ref), (g2_ref, w2_ref))):
         for q in range(7):
             base = q * 3 * C
@@ -430,44 +449,34 @@
             )
             copy.start()
             copies.append(copy)
-    below, above, has_below, has_above = tile_neighbours()
-    total[...] = own_ref[...]
-    for j in range(KB):
-        total[slo_ref[0, j]] += flo_ref[j] * jnp.where(has_below, 1.0, 0.0)
-        total[shi_ref[0, j]] += fhi_ref[j] * jnp.where(has_above, 1.0, 0.0)
-    rounded[...] = total[...].astype(BF16)
-    copy = pltpu.make_async_copy(rounded, fg_ref, last)
-    copy.start()
-    for copy in copies + [copy]:
+    for copy in copies:
         copy.wait()
 
 
-def finish(slo, shi, own, flo, fhi, g1, g2):
+def finish(grad, g1, g2):
     kern = jax.ShapeDtypeStruct((K, C, C), F32)
     return pl.pallas_call(
         finish_kernel,
         out_shape=(jax.ShapeDtypeStruct((NB, C, ROW), BF16), kern, kern),
-        in_specs=[SMEM] * 2 + [VMEM] * 5,
+        in_specs=[VMEM] * 3,
         out_specs=(HBM,) * 3,
         scratch_shapes=[
-            pltpu.VMEM((NB, C, ROW), F32),
-            pltpu.VMEM((NB, C, ROW), BF16),
             pltpu.VMEM((2, K, C, C), F32),
             pltpu.SemaphoreType.DMA((2, 7)),
             pltpu.SemaphoreType.DMA,
         ],
         compiler_params=pltpu.CompilerParams(vmem_limit_bytes=VMEM_LIMIT),
         name="finish",
-    )(slo, shi, own, flo, fhi, g1, g2)
+    )(grad, g1, g2)
 
 
 def body(ny, nz, nx, features, pre_act, out_grad, weight_one, weight_two, block_count, pair_in, pair_off,
          row_map, send_lo, send_hi):
-    operands = (features, pre_act, out_grad, weight_one, weight_two, block_count, pair_in, pair_off,
+    operands = (features, pre_act, out_grad, weight_one, weight_two, block_count.reshape(1, 1), pair_in, pair_off,
                 row_map, send_lo, send_hi)
-    operands = [a if a.shape == (1,) else pltpu.with_memory_space_constraint(a, pltpu.HBM) for a in operands]
-    g1, g2, own, xlo, xhi = fused(ny, nz, nx, *operands)
-    return finish(send_lo, send_hi, own, xlo, xhi, g1, g2)
+    operands = [a if a.size == 1 else pltpu.with_memory_space_constraint(a, pltpu.HBM) for a in operands]
+    g1, g2, grad = fused(ny, nz, nx, *operands)
+    return finish(grad, g1, g2)
 
 
 def solution(mesh):

time: 63.2 us -> 56.7 us (0.90)
  Pallas kernels: 61.7 us -> 55.3 us
    pallas_call x1, Pallas kernels: 59.4 us -> 53.6 us  [fused(): pl.pallas_call(functools.partial(fused_kernel, ny, nz, nx), out_shape=(pa...]
where the time goes in v4:
time: 56.7 us; the launch traced here: 56.6 us
  Pallas kernels  55.3 us (98%)
  between operations  1.29 us (2%)
    pallas_call x1, Pallas kernels, fused(): pl.pallas_call(functools.partial(fused_kernel, ny, nz, nx), out_shape=(pa...  53.6 us
    pallas_call x1, Pallas kernels, finish(): pl.pallas_call(finish_kernel, out_shape=(jax.ShapeDtypeStruct((NB, C, ROW...  1.71 us

profile of v4, /device:TPU:1, one launch (start us, length us, event | category | flops | bytes accessed | tf_op | source)
XLA Modules:
  0.0 56.6 jit_solution(5270513134064580973)
XLA Ops:
  1.3 53.6 %fused.1 = (bf16[2048,128]{1,0:T(8,128)(2,1)S(1)}, bf16[2048,128]{1,0:T(8,128)(2,1)S(1)}, bf16[4,96,128]{2,1,0:T(8,128)(2,1)S(1)}) custom-call(bf16[4,96,128]{2,1,0:T(8,128)(2,1)} %refs_0_.1, bf16[4,96,128]{2,1,0:T(8,128)(2,1)} %refs_1_.1, bf16[4,96,128]{2,1,0:T(8,128)(2,1)} %refs_2_.1, bf16[27,96,96]{2,1,0:T(8,128)(2,1)} %refs_3_.1, ...), custom_call_target="tpu_custom_call" | custom-call | tf_op jit(solution)/shard_map/fused/pallas_call | solution.py:376
  54.8 1.7 %finish.1 = (bf16[4,96,128]{2,1,0:T(8,128)(2,1)}, f32[27,96,96]{2,1,0:T(8,128)}, f32[27,96,96]{2,1,0:T(8,128)}) custom-call(bf16[4,96,128]{2,1,0:T(8,128)(2,1)S(1)} %get-tuple-element.6.grad_ref, bf16[2048,128]{1,0:T(8,128)(2,1)S(1)} %get-tuple-element.7.g1_ref, bf16[2048,128]{1,0:T(8,128)(2,1)S(1)} %get-tuple-element.8.g2_ref), custom_call_target="tpu_custom_call" | custom-call | tf_op jit(solution)/shard_map/finish/pallas_call | solution.py:458

commit v5 on v4

--- a/solution.py
+++ b/solution.py
@@ -15,12 +15,12 @@
 ROW = 128
 EXT = NB + 2 * KB
 PAIRS = NB * PB
-UNROLL = 32
+UNROLL = 64
 NT = (((1,), (1,)), ((), ()))
 PACKED = 2048
 F32 = jnp.float32
 BF16 = jnp.bfloat16
-VMEM_LIMIT = 24 * 1024 * 1024
+VMEM_LIMIT = 28 * 1024 * 1024
 
 HBM = pl.BlockSpec(memory_space=pltpu.HBM)
 VMEM = pl.BlockSpec(memory_space=pltpu.VMEM)
@@ -74,6 +74,15 @@
         return carry
 
     lax.fori_loop(0, NB, block, 0)
+
+
+def scatter_columns(rmap, count, grads, h):
+    lane = lax.broadcasted_iota(jnp.int32, (ROW, ROW), 1)
+    pair = lax.broadcasted_iota(jnp.int32, (PAIRS, ROW), 0)
+    columns = jnp.transpose(rmap[0] + jnp.where(pair < count * PB, 0, 2 * ROW))
+    for p in range(PAIRS):
+        picks = jnp.where(columns[:, p : p + 1] == lane, 1.0, 0.0).astype(BF16)
+        h[p] = jnp.dot(grads[p // PB], picks, preferred_element_type=F32).astype(BF16)
 
 
 def scatter_grads(picks, gt, ht):
@@ -120,18 +129,15 @@
 def pack(table, sums, packed):
     lane = lax.broadcasted_iota(jnp.int32, (C, ROW), 1)
 
-    def group(q, carry):
+    for q in range(7):
         a = sum_of(4 * q, 0, table, sums)
         b = pltpu.roll(sum_of(4 * q + 1, 0, table, sums), 96, 1)
         c = pltpu.roll(sum_of(4 * q + 2, 0, table, sums), 64, 1)
         d = pltpu.roll(sum_of(4 * q + 3, 0, table, sums), 32, 1)
-        base = pl.multiple_of(q * 3 * C, 3 * C)
+        base = q * 3 * C
         packed[pl.ds(base, C), :] = jnp.where(lane < 96, a, b)
         packed[pl.ds(base + C, C), :] = jnp.where(lane < 64, b, c)
         packed[pl.ds(base + 2 * C, C), :] = jnp.where(lane < 32, c, d)
-        return carry
-
-    lax.fori_loop(0, 7, group, 0)
     packed[21 * C :, :] = jnp.zeros((PACKED - 21 * C, ROW), F32)
 
 
@@ -201,11 +207,8 @@
     to_scalar.start()
     loads["rmap"].wait()
     loads["count"].wait()
-    build_picks(rmap, count[0, 0], picks)
     loads["og"].wait()
-    for b in range(NB):
-        gt[b, :, 0:C] = jnp.transpose(og[b])
-    scatter_grads(picks, gt, ht)
+    scatter_columns(rmap, count[0, 0], og, gathered)
 
     for name in ("slo", "shi", "pre", "feat"):
         loads[name].wait()
@@ -218,7 +221,7 @@
         loads[name].wait()
     to_scalar.wait()
     running_sums(
-        lambda p: lax.dot_general(w2[poff[0, p]], ht[p, :, 0:C], NT, preferred_element_type=F32),
+        lambda p: jnp.dot(w2[poff[0, p]], gathered[p], preferred_element_type=F32),
         3, pin, table, sums,
     )
     for j in range(KB):
@@ -239,6 +242,11 @@
     )
     for copy in list(halo[1]) + list(back) + list(halo[0]):
         copy.start()
+
+    build_picks(rmap, count[0, 0], picks)
+    for b in range(NB):
+        gt[b, :, 0:C] = jnp.transpose(og[b])
+    scatter_grads(picks, gt, ht)
 
     def extend(f, own, ext):
         ext[0:NB] = own

time: 56.7 us -> 56 us (0.988)
  Pallas kernels: 55.3 us -> 54.5 us
    pallas_call x1, Pallas kernels: 53.6 us -> 52.8 us  [fused(): pl.pallas_call(functools.partial(fused_kernel, ny, nz, nx), out_shape=(pa...]
where the time goes in v5:
time: 56 us; the launch traced here: 55.8 us
  Pallas kernels  54.5 us (97%)
  between operations  1.29 us (2%)
    pallas_call x1, Pallas kernels, fused(): pl.pallas_call(functools.partial(fused_kernel, ny, nz, nx), out_shape=(pa...  52.8 us
    pallas_call x1, Pallas kernels, finish(): pl.pallas_call(finish_kernel, out_shape=(jax.ShapeDtypeStruct((NB, C, ROW...  1.71 us

profile of v5, /device:TPU:1, one launch (start us, length us, event | category | flops | bytes accessed | tf_op | source)
XLA Modules:
  0.0 55.8 jit_solution(412732556969365864)
XLA Ops:
  1.3 52.8 %fused.1 = (bf16[2048,128]{1,0:T(8,128)(2,1)S(1)}, bf16[2048,128]{1,0:T(8,128)(2,1)S(1)}, bf16[4,96,128]{2,1,0:T(8,128)(2,1)S(1)}) custom-call(bf16[4,96,128]{2,1,0:T(8,128)(2,1)} %refs_0_.1, bf16[4,96,128]{2,1,0:T(8,128)(2,1)} %refs_1_.1, bf16[4,96,128]{2,1,0:T(8,128)(2,1)} %refs_2_.1, bf16[27,96,96]{2,1,0:T(8,128)(2,1)} %refs_3_.1, ...), custom_call_target="tpu_custom_call" | custom-call | tf_op jit(solution)/shard_map/fused/pallas_call | solution.py:384
  54.1 1.7 %finish.1 = (bf16[4,96,128]{2,1,0:T(8,128)(2,1)}, f32[27,96,96]{2,1,0:T(8,128)}, f32[27,96,96]{2,1,0:T(8,128)}) custom-call(bf16[4,96,128]{2,1,0:T(8,128)(2,1)S(1)} %get-tuple-element.6.grad_ref, bf16[2048,128]{1,0:T(8,128)(2,1)S(1)} %get-tuple-element.7.g1_ref, bf16[2048,128]{1,0:T(8,128)(2,1)S(1)} %get-tuple-element.8.g2_ref), custom_call_target="tpu_custom_call" | custom-call | tf_op jit(solution)/shard_map/finish/pallas_call | solution.py:466

commit v6 on v5

--- a/solution.py
+++ b/solution.py
@@ -217,18 +217,6 @@
         out_hi[0, j] = jnp.maximum(pre[shi[0, j]], 0.0)
         out_lo[1, j] = feat[slo[0, j]]
         out_hi[1, j] = feat[shi[0, j]]
-    for name in ("pin", "poff", "w2"):
-        loads[name].wait()
-    to_scalar.wait()
-    running_sums(
-        lambda p: jnp.dot(w2[poff[0, p]], gathered[p], preferred_element_type=F32),
-        3, pin, table, sums,
-    )
-    for j in range(KB):
-        gb_lo[j] = sum_of(NB + j, 3, table, sums).astype(gb_lo.dtype)
-        gb_hi[j] = sum_of(NB + KB + j, 3, table, sums).astype(gb_hi.dtype)
-    for b in range(NB):
-        own[b] = sum_of(b, 3, table, sums)
     pl.semaphore_wait(barrier, len(peers))
     halo = []
     for f in range(2):
@@ -236,11 +224,26 @@
             remote(out_hi.at[f], in_lo.at[f], hs.at[0, f], hr.at[0, f], above),
             remote(out_lo.at[f], in_hi.at[f], hs.at[1, f], hr.at[1, f], below),
         ))
+    for copy in list(halo[0]) + list(halo[1]):
+        copy.start()
+
+    for name in ("pin", "poff", "w2"):
+        loads[name].wait()
+    to_scalar.wait()
+    running_sums(
+        lambda p: jnp.dot(w2[poff[0, p]], gathered[p], preferred_element_type=F32),
+        3, pin, table, sums,
+    )
+    for j in range(KB):
+        gb_lo[j] = sum_of(NB + j, 3, table, sums).astype(gb_lo.dtype)
+        gb_hi[j] = sum_of(NB + KB + j, 3, table, sums).astype(gb_hi.dtype)
+    for b in range(NB):
+        own[b] = sum_of(b, 3, table, sums)
     back = (
         remote(gb_hi, fb_lo, gs.at[0], gr.at[0], above),
         remote(gb_lo, fb_hi, gs.at[1], gr.at[1], below),
     )
-    for copy in list(halo[1]) + list(back) + list(halo[0]):
+    for copy in back:
         copy.start()
 
     build_picks(rmap, count[0, 0], picks)
@@ -316,6 +319,12 @@
             total = total + from_below * lo[j].astype(F32) + from_above * hi[j].astype(F32)
         return total
 
+    extend(0, jnp.maximum(pre[...], 0.0), ext_h)
+    running_sums(
+        lambda p: jnp.dot(ext_h[pin[0, p]], ht[p], preferred_element_type=F32), 0, poff, table, sums
+    )
+    pack(table, sums, dwp.at[1])
+    swap_halves(1)
     extend(1, feat[...], ext_x)
     gather_rows(picks, pin, ext_x, gathered)
     for copy in back:
@@ -329,14 +338,8 @@
     pack(table, sums, dwp.at[0])
     swap_halves(0)
 
-    extend(0, jnp.maximum(pre[...], 0.0), ext_h)
-    running_sums(
-        lambda p: jnp.dot(ext_h[pin[0, p]], ht[p], preferred_element_type=F32), 0, poff, table, sums
-    )
-    pack(table, sums, dwp.at[1])
-    swap_halves(1)
+    scatter_plane(1)
     scatter_plane(0)
-    scatter_plane(1)
 
     scatter_grads(picks, gt, ht)
     loads["w1"].wait()
@@ -350,22 +353,22 @@
     for b in range(NB):
         own[b] = sum_of(b, 3, table, sums)
 
+    exchange_line(1)
     exchange_line(0)
-    exchange_line(1)
     last = (
         remote(gb2_hi, fb2_lo, g2s.at[0], g2r.at[0], above),
         remote(gb2_lo, fb2_hi, g2s.at[1], g2r.at[1], below),
     )
     for copy in last:
         copy.start()
+    gather_plane(1)
     gather_plane(0)
-    gather_plane(1)
     for copy in last:
         copy.wait()
     for b in range(NB):
         fg_ref[b] = add_back(b, own[b], fb2_lo, fb2_hi).astype(BF16)
+    share_halves(1)
     share_halves(0)
-    share_halves(1)
     settle(0)
     settle(1)
 

time: 56 us -> 56.4 us (level)
  no operation moved by 1% of the time
where the time goes in v6:
time: 56.4 us; the launch traced here: 55.8 us
  Pallas kernels  54.5 us (97%)
  between operations  1.29 us (2%)
    pallas_call x1, Pallas kernels, fused(): pl.pallas_call(functools.partial(fused_kernel, ny, nz, nx), out_shape=(pa...  52.8 us
    pallas_call x1, Pallas kernels, finish(): pl.pallas_call(finish_kernel, out_shape=(jax.ShapeDtypeStruct((NB, C, ROW...  1.71 us

profile of v6, /device:TPU:1, one launch (start us, length us, event | category | flops | bytes accessed | tf_op | source)
XLA Modules:
  0.0 55.8 jit_solution(3828118081420109905)
XLA Ops:
  1.3 52.8 %fused.1 = (bf16[2048,128]{1,0:T(8,128)(2,1)S(1)}, bf16[2048,128]{1,0:T(8,128)(2,1)S(1)}, bf16[4,96,128]{2,1,0:T(8,128)(2,1)S(1)}) custom-call(bf16[4,96,128]{2,1,0:T(8,128)(2,1)} %refs_0_.1, bf16[4,96,128]{2,1,0:T(8,128)(2,1)} %refs_1_.1, bf16[4,96,128]{2,1,0:T(8,128)(2,1)} %refs_2_.1, bf16[27,96,96]{2,1,0:T(8,128)(2,1)} %refs_3_.1, ...), custom_call_target="tpu_custom_call" | custom-call | tf_op jit(solution)/shard_map/fused/pallas_call | solution.py:387
  54.1 1.7 %finish.1 = (bf16[4,96,128]{2,1,0:T(8,128)(2,1)}, f32[27,96,96]{2,1,0:T(8,128)}, f32[27,96,96]{2,1,0:T(8,128)}) custom-call(bf16[4,96,128]{2,1,0:T(8,128)(2,1)S(1)} %get-tuple-element.6.grad_ref, bf16[2048,128]{1,0:T(8,128)(2,1)S(1)} %get-tuple-element.7.g1_ref, bf16[2048,128]{1,0:T(8,128)(2,1)S(1)} %get-tuple-element.8.g2_ref), custom_call_target="tpu_custom_call" | custom-call | tf_op jit(solution)/shard_map/finish/pallas_call | solution.py:469

commit v7 on v5

--- a/solution.py
+++ b/solution.py
@@ -159,30 +159,33 @@
     below, above, has_below, has_above = tile_neighbours()
     other = (district + 1 - 2 * core, tile)
 
-    def plane_of(n, me, device):
+    def across(flip, first, i, j):
+        over_y = ((i * 2 + core), (z * nx + j))
+        over_z = (district, (i * nx + j))
+        along = 1 - flip if first else flip
+        return tuple(a * along + b * (1 - along) for a, b in zip(over_y, over_z))
+
+    def plane_of(flip):
+        me = y * (1 - flip) + z * flip
         steps = sorted(
-            [(a, b) for a in range(n) for b in range(nx) if a + b],
-            key=lambda step: -min(step[0], n - step[0]) - min(step[1], nx - step[1]),
+            [(a, b) for a in range(ny) for b in range(nx) if a + b],
+            key=lambda step: -min(step[0], ny - step[0]) - min(step[1], nx - step[1]),
         )
-        places = [(lax.rem(me + a, n), lax.rem(x + b, nx)) for a, b in steps]
-        return [i * nx + j for i, j in places], [device(i, j) for i, j in places]
-
-    def line_of(n, me, device):
-        order = sorted(range(1, n), key=lambda a: -min(a, n - a))
-        return [device(lax.rem(me + a, n), x) for a in order]
-
-    def over_y(i, j):
-        return (i * 2 + core, z * nx + j)
-
-    def over_z(i, j):
-        return (district, i * nx + j)
-
-    planes = (plane_of(ny, y, over_y), plane_of(nz, z, over_z))
-    lines = (line_of(nz, z, over_z), line_of(ny, y, over_y))
-    own_part = (y * nx + x, z * nx + x)
-    own_slot = (z, y)
-    parts = (half // (ny * nx), half // (nz * nx))
-    slots = (nz, ny)
+        places = [(lax.rem(me + a, ny), lax.rem(x + b, nx)) for a, b in steps]
+        return [i * nx + j for i, j in places], [across(flip, True, i, j) for i, j in places]
+
+    def line_of(flip):
+        me = y * flip + z * (1 - flip)
+        order = sorted(range(1, nz), key=lambda a: -min(a, nz - a))
+        return [across(flip, False, lax.rem(me + a, nz), x) for a in order]
+
+    flips = (core, 1 - core)
+    planes = [plane_of(flip) for flip in flips]
+    lines = [line_of(flip) for flip in flips]
+    own_part = [(y * (1 - flip) + z * flip) * nx + x for flip in flips]
+    own_slot = [y * flip + z * (1 - flip) for flip in flips]
+    parts = (half // (ny * nx),) * 2
+    slots = (nz, nz)
 
     loads = {}
     pieces = (("rmap", rmap_in, rmap), ("count", count_in, count), ("poff_v", poff_in, poff_v), ("pin_v", pin_in, pin_v),
@@ -192,8 +195,7 @@
         loads[name] = pltpu.make_async_copy(src, dst, load.at[i])
         loads[name].start()
     barrier = pltpu.get_barrier_semaphore()
-    peers = planes[0][1] + [other, below, above]
-    peers += [over_z(lax.rem(z + a, nz), lax.rem(x + b, nx)) for a in range(1, nz) for b in range(nx)]
+    peers = planes[0][1] + planes[1][1] + [other, below, above]
     for peer in peers:
         pl.semaphore_signal(barrier, inc=1, device_id=peer, device_id_type=pl.DeviceIdType.MESH)
 

time: 56 us -> 56.2 us (level)
  no operation moved by 1% of the time
where the time goes in v7:
time: 56.2 us; the launch traced here: 56.1 us
  Pallas kernels  54.8 us (98%)
  between operations  1.29 us (2%)
    pallas_call x1, Pallas kernels, fused(): pl.pallas_call(functools.partial(fused_kernel, ny, nz, nx), out_shape=(pa...  53.1 us
    pallas_call x1, Pallas kernels, finish(): pl.pallas_call(finish_kernel, out_shape=(jax.ShapeDtypeStruct((NB, C, ROW...  1.71 us

profile of v7, /device:TPU:1, one launch (start us, length us, event | category | flops | bytes accessed | tf_op | source)
XLA Modules:
  0.0 56.1 jit_solution(10280050666211270153)
XLA Ops:
  1.3 53.1 %fused.1 = (bf16[2048,128]{1,0:T(8,128)(2,1)S(1)}, bf16[2048,128]{1,0:T(8,128)(2,1)S(1)}, bf16[4,96,128]{2,1,0:T(8,128)(2,1)S(1)}) custom-call(bf16[4,96,128]{2,1,0:T(8,128)(2,1)} %refs_0_.1, bf16[4,96,128]{2,1,0:T(8,128)(2,1)} %refs_1_.1, bf16[4,96,128]{2,1,0:T(8,128)(2,1)} %refs_2_.1, bf16[27,96,96]{2,1,0:T(8,128)(2,1)} %refs_3_.1, ...), custom_call_target="tpu_custom_call" | custom-call | tf_op jit(solution)/shard_map/fused/pallas_call | solution.py:386
  54.4 1.7 %finish.1 = (bf16[4,96,128]{2,1,0:T(8,128)(2,1)}, f32[27,96,96]{2,1,0:T(8,128)}, f32[27,96,96]{2,1,0:T(8,128)}) custom-call(bf16[4,96,128]{2,1,0:T(8,128)(2,1)S(1)} %get-tuple-element.6.grad_ref, bf16[2048,128]{1,0:T(8,128)(2,1)S(1)} %get-tuple-element.7.g1_ref, bf16[2048,128]{1,0:T(8,128)(2,1)S(1)} %get-tuple-element.8.g2_ref), custom_call_target="tpu_custom_call" | custom-call | tf_op jit(solution)/shard_map/finish/pallas_call | solution.py:468

commit v8 on v5

--- a/solution.py
+++ b/solution.py
@@ -147,7 +147,7 @@
      feat, pre, og, w1, w2, rmap, pin_v, poff_v, count, pin, poff, slo, shi, table_v, table,
      picks, gt, ht, gathered, sums, ext_h, ext_x, own,
      out_lo, out_hi, in_lo, in_hi, gb_lo, gb_hi, fb_lo, fb_hi, gb2_lo, gb2_hi, fb2_lo, fb2_hi,
-     dwp, rcv0, snd1, rcv1, mine, gat3, fin1,
+     dwp, snd0, rcv0, snd1, rcv1, mine, gat3, fin1,
      load, tsem, hs, hr, gs, gr, g2s, g2r, s0, r0, s1, r1, s3, r3, s5, r5, s6, r6) = refs
     half = PACKED // 2
     district = lax.axis_index("district")
@@ -261,17 +261,18 @@
     outs = (g1_ref, g2_ref)
 
     def swap_halves(g):
-        remote(dwp.at[g, away, :], rcv0.at[g], s0.at[g], r0.at[g], other).start()
+        snd0[g] = dwp[g, away, :].astype(BF16)
+        remote(snd0.at[g], rcv0.at[g], s0.at[g], r0.at[g], other).start()
 
     def scatter_plane(g):
         wait_all(rcv0.at[g], r0.at[g])
-        snd1[g] = (dwp[g, keep, :] + rcv0[g]).astype(BF16)
+        snd1[g] = (dwp[g, keep, :] + rcv0[g].astype(F32)).astype(BF16)
         part = parts[g]
         for s, (index, peer) in enumerate(zip(*planes[g])):
             rows = pl.ds(pl.multiple_of(index * part, part), part)
             remote(snd1.at[g, rows, :], rcv1.at[g, s, 0:part], s1.at[g], r1.at[g], peer).start()
         at = pl.ds(pl.multiple_of(core * half + own_part[g] * part, part), part)
-        mine[g, 0:part] = dwp[g, at, :] + rcv0[g, chunks[g], :]
+        mine[g, 0:part] = dwp[g, at, :] + rcv0[g, chunks[g], :].astype(F32)
 
     def exchange_line(g):
         part = parts[g]
@@ -412,7 +413,8 @@
             pltpu.VMEM((2, KB, C, ROW), BF16),
             four, four, four, four, four_wide, four_wide, four_wide, four_wide,
             pltpu.VMEM((2, PACKED, ROW), F32),
-            pltpu.VMEM((2, half, ROW), F32),
+            pltpu.VMEM((2, half, ROW), BF16),
+            pltpu.VMEM((2, half, ROW), BF16),
             pltpu.VMEM((2, half, ROW), BF16),
             pltpu.VMEM((2, near, part, ROW), BF16),
             pltpu.VMEM((2, part, ROW), F32),

time: 56 us -> 55.8 us (level)
  no operation moved by 1% of the time
where the time goes in v8:
time: 55.8 us; the launch traced here: 55.7 us
  Pallas kernels  54.4 us (97%)
  between operations  1.29 us (2%)
    pallas_call x1, Pallas kernels, fused(): pl.pallas_call(functools.partial(fused_kernel, ny, nz, nx), out_shape=(pa...  52.7 us
    pallas_call x1, Pallas kernels, finish(): pl.pallas_call(finish_kernel, out_shape=(jax.ShapeDtypeStruct((NB, C, ROW...  1.71 us

profile of v8, /device:TPU:1, one launch (start us, length us, event | category | flops | bytes accessed | tf_op | source)
XLA Modules:
  0.0 55.7 jit_solution(4942497803159358513)
XLA Ops:
  1.3 52.7 %fused.1 = (bf16[2048,128]{1,0:T(8,128)(2,1)S(1)}, bf16[2048,128]{1,0:T(8,128)(2,1)S(1)}, bf16[4,96,128]{2,1,0:T(8,128)(2,1)S(1)}) custom-call(bf16[4,96,128]{2,1,0:T(8,128)(2,1)} %refs_0_.1, bf16[4,96,128]{2,1,0:T(8,128)(2,1)} %refs_1_.1, bf16[4,96,128]{2,1,0:T(8,128)(2,1)} %refs_2_.1, bf16[27,96,96]{2,1,0:T(8,128)(2,1)} %refs_3_.1, ...), custom_call_target="tpu_custom_call" | custom-call | tf_op jit(solution)/shard_map/fused/pallas_call | solution.py:385
  54.0 1.7 %finish.1 = (bf16[4,96,128]{2,1,0:T(8,128)(2,1)}, f32[27,96,96]{2,1,0:T(8,128)}, f32[27,96,96]{2,1,0:T(8,128)}) custom-call(bf16[4,96,128]{2,1,0:T(8,128)(2,1)S(1)} %get-tuple-element.6.grad_ref, bf16[2048,128]{1,0:T(8,128)(2,1)S(1)} %get-tuple-element.7.g1_ref, bf16[2048,128]{1,0:T(8,128)(2,1)S(1)} %get-tuple-element.8.g2_ref), custom_call_target="tpu_custom_call" | custom-call | tf_op jit(solution)/shard_map/finish/pallas_call | solution.py:468
